TPU v7x, 256 devices: a whole 4x4x8 slice. The times are simulated.
256 devices in a mesh: ctx: 16 (over z_hi, x), head: 16 (over y, z_lo, core).
Axes of the slice: x: 4, y: 4, z: 8 (z_hi: 4, z_lo: 2; z = z_hi * 2 + z_lo), core: 2. Of those that a mesh axis runs over, the one named last changes fastest.
Arguments:
- queries: bfloat16 [2048, 12288], P('ctx', 'head'), may hold values from -12 to 12
- latent: bfloat16 [2048, 512], P('ctx'), may hold values from -6 to 6
- rope_key: bfloat16 [2048, 64], P('ctx'), may hold values from -12 to 12
- key_weight: bfloat16 [512, 8192], P(None, 'head'), may hold values from -0.25 to 0.25
- value_weight: bfloat16 [512, 8192], P(None, 'head'), may hold values from -0.25 to 0.25
- lambda_pair: float32 [32], P('head'), may hold values from 0.2 to 0.8
- norm_gain: float32 [8192], P('head'), may hold values from 0.1 to 1.9
- out_grad: bfloat16 [2048, 8192], P('ctx', 'head'), may hold values from -6 to 6
- block_order: int32 [32], replicated, may hold values from 0 to 31, as said below
Outputs:
- query_grad: bfloat16 [2048, 12288], P('ctx', 'head')
- latent_grad: bfloat16 [2048, 512], P('ctx')
- rope_grad: bfloat16 [2048, 64], P('ctx')
Inputs may be any that keep to these rules, and one draw needn't show every extreme that they name: `block_order`: slots 2d and 2d + 1 hold blocks b and 31 - b with b < 16; every block appears once.
All inputs are finite; a program needn't handle non-finite values.
Results may differ from a plain program's by a relative error of at most 0.03.
Values may be sent and summed in bfloat16 or wider, within the bound.
A program may use at most 64 MiB of HBM per device.

v0:
```python
import jax
import jax.numpy as jnp
from jax import lax
from jax.sharding import PartitionSpec as P

D_LAT = 512
D_NOPE = 128
D_ROPE = 64
VALUE_WIDTH = 128


eps = 1e-06


def passed_along(value, axis, steps):
    count = lax.axis_size(axis)
    pairs = [(source, (source + steps) % count) for source in range(count)]
    return lax.ppermute(value, axis, pairs)


def slot_positions(block_order, row_ids, half_rows):
    slot_ids = row_ids // half_rows
    table = slot_ids[:, None] == jnp.arange(block_order.shape[0], dtype=jnp.int32)[None, :]
    return (
        jnp.sum(jnp.where(table, block_order[None, :], 0), axis=1) * half_rows + row_ids % half_rows
    )


def score_tile(query_heads, key_nope, key_rope, logit_scale):
    nope_part = jnp.einsum(
        "ihd,khd->hik", query_heads[:, :, :D_NOPE], key_nope, preferred_element_type=jnp.float32
    )
    rope_part = jnp.einsum(
        "ihd,kd->hik", query_heads[:, :, D_NOPE:], key_rope, preferred_element_type=jnp.float32
    )
    return logit_scale * (nope_part + rope_part)


def online_update(
    running, query_heads, query_pos, key_nope, key_values, key_rope, key_pos, logit_scale
):
    top_run, total_run, output_run = running
    scores = score_tile(query_heads, key_nope, key_rope, logit_scale)
    scores = jnp.where(key_pos[None, None, :] <= query_pos[None, :, None], scores, -jnp.inf)
    top_new = jnp.maximum(top_run, jnp.max(scores, axis=2))
    rescale = jnp.exp(top_run - top_new)
    weights = jnp.exp(scores - top_new[:, :, None])
    total_new = jnp.sum(weights, axis=2)
    pair_count = key_values.shape[1]
    head_count, rows_dev, key_count = weights.shape
    paired = weights.astype(jnp.bfloat16).reshape(pair_count, 2, rows_dev, key_count)
    added = jnp.einsum("pmik,kpe->pmie", paired, key_values, preferred_element_type=jnp.float32)
    output_new = output_run * rescale.reshape(pair_count, 2, rows_dev, 1) + added
    return (top_new, total_new, output_new)


def tile_grads(query_side, key_nope, key_values, key_rope, key_pos, factor, logit_scale):
    query_heads, gradient_lowered, log_total, delta_rows, query_pos = query_side
    scores = score_tile(query_heads, key_nope, key_rope, logit_scale)
    visible = key_pos[None, None, :] <= query_pos[None, :, None]
    probabilities = jnp.where(visible, jnp.exp(scores - log_total[:, :, None]), 0.0)
    head_count, rows_dev, key_count = probabilities.shape
    pair_count = head_count // 2
    through_values = jnp.einsum(
        "pie,kpe->pik", gradient_lowered, key_values, preferred_element_type=jnp.float32
    )
    paired = probabilities.reshape(pair_count, 2, rows_dev, key_count)
    d_paired = paired * (
        factor[:, :, None, None] * through_values[:, None]
        - delta_rows.reshape(pair_count, 2, rows_dev, 1)
    )
    scores_gradient = d_paired.reshape(head_count, rows_dev, key_count).astype(jnp.bfloat16)
    merged_scores = jnp.sum(paired * factor[:, :, None, None], axis=1).astype(jnp.bfloat16)
    value_grad = jnp.einsum(
        "pik,pie->kpe", merged_scores, gradient_lowered, preferred_element_type=jnp.float32
    )
    query_nope = jnp.einsum(
        "hik,khd->ihd", scores_gradient, key_nope, preferred_element_type=jnp.float32
    )
    query_rope = jnp.einsum(
        "hik,kd->ihd", scores_gradient, key_rope, preferred_element_type=jnp.float32
    )
    query_part = logit_scale * jnp.concatenate([query_nope, query_rope], axis=2)
    key_grad = logit_scale * jnp.einsum(
        "hik,ihd->khd", scores_gradient, query_heads, preferred_element_type=jnp.float32
    )
    return (
        query_part,
        key_grad[:, :, :D_NOPE],
        jnp.sum(key_grad[:, :, D_NOPE:], axis=1),
        value_grad,
    )


def latent_terms(nope_grad, value_grad, key_weight, value_weight):
    row_count = nope_grad.shape[0]
    nope_flat = nope_grad.astype(jnp.bfloat16).reshape(row_count, -1)
    value_flat = value_grad.astype(jnp.bfloat16).reshape(row_count, -1)
    from_keys = jnp.einsum("kc,lc->kl", nope_flat, key_weight, preferred_element_type=jnp.float32)
    from_values = jnp.einsum(
        "kc,lc->kl", value_flat, value_weight, preferred_element_type=jnp.float32
    )
    return from_keys + from_values


def on_device(
    queries,
    latent,
    rope_key,
    key_weight,
    value_weight,
    lambda_pair,
    norm_gain,
    out_grad,
    block_order,
):
    logit_scale = (D_NOPE + D_ROPE) ** (-0.5)
    ctx_count = lax.axis_size("ctx")
    my_index = lax.axis_index("ctx")
    rows_dev = queries.shape[0]
    half_rows = rows_dev // 2
    head_count = key_weight.shape[1] // D_NOPE
    pair_count = head_count // 2
    query_heads = queries.reshape(rows_dev, head_count, D_NOPE + D_ROPE)
    row_index = jnp.arange(rows_dev, dtype=jnp.int32)
    query_pos = slot_positions(block_order, my_index * rows_dev + row_index, half_rows)
    factor = jnp.stack([jnp.ones_like(lambda_pair), -lambda_pair], axis=1)

    def expand(key_block):
        row_count = key_block.shape[0]
        key_nope = jnp.dot(key_block, key_weight, preferred_element_type=jnp.float32).astype(
            jnp.bfloat16
        )
        key_values = jnp.dot(key_block, value_weight, preferred_element_type=jnp.float32).astype(
            jnp.bfloat16
        )
        return (
            key_nope.reshape(row_count, head_count, D_NOPE),
            key_values.reshape(row_count, pair_count, 2 * VALUE_WIDTH),
        )

    start_state = (
        jnp.full((head_count, rows_dev), -1e30, jnp.float32),
        jnp.zeros((head_count, rows_dev), jnp.float32),
        jnp.zeros((pair_count, 2, rows_dev, 2 * VALUE_WIDTH), jnp.float32),
    )
    key_block = lax.all_gather(latent, "ctx", axis=0, tiled=True)
    key_rope = lax.all_gather(rope_key, "ctx", axis=0, tiled=True)
    row_count = key_rope.shape[0]
    key_nope, key_values = expand(key_block)
    key_pos = slot_positions(block_order, jnp.arange(row_count, dtype=jnp.int32), half_rows)
    finished = online_update(
        start_state, query_heads, query_pos, key_nope, key_values, key_rope, key_pos, logit_scale
    )
    top_run, total_run, output_run = finished
    maps_out = output_run / total_run.reshape(pair_count, 2, rows_dev, 1)
    log_total = top_run + jnp.log(total_run)
    mixed_out = maps_out[:, 0] - lambda_pair[:, None, None] * maps_out[:, 1]
    root_mean = jnp.sqrt(jnp.mean(mixed_out * mixed_out, axis=2, keepdims=True) + eps)
    normed = mixed_out / root_mean
    grad_view = (
        out_grad.reshape(rows_dev, pair_count, 2 * VALUE_WIDTH)
        .transpose(1, 0, 2)
        .astype(jnp.float32)
    )
    scaled = grad_view * norm_gain.reshape(pair_count, 1, 2 * VALUE_WIDTH)
    d_mixed = (scaled - normed * jnp.mean(scaled * normed, axis=2, keepdims=True)) / root_mean
    gradient_lowered = d_mixed.astype(jnp.bfloat16)
    delta_rows = (factor[:, :, None] * jnp.sum(d_mixed[:, None] * maps_out, axis=3)).reshape(
        head_count, rows_dev
    )
    full_side = (query_heads, gradient_lowered, log_total, delta_rows, query_pos)

    def run_tiles(query_side, key_nope, key_values, key_rope, key_pos):
        query_part, nope_grad, rope_part, value_grad = tile_grads(
            query_side, key_nope, key_values, key_rope, key_pos, factor, logit_scale
        )
        return (
            query_part,
            latent_terms(nope_grad, value_grad, key_weight, value_weight),
            rope_part,
        )

    def key_grads(key_nope, key_values, key_rope, key_pos):
        return run_tiles(full_side, key_nope, key_values, key_rope, key_pos)

    zero_query = jnp.zeros((rows_dev, head_count, D_NOPE + D_ROPE), jnp.float32)

    def visit_block(turn_index, state_now):
        key_block, key_rope, latent_acc, rope_acc, query_acc = state_now
        source = (my_index - turn_index) % ctx_count
        key_pos = slot_positions(block_order, source * rows_dev + row_index, half_rows)
        key_nope, key_values = expand(key_block)
        query_part, latent_part, rope_part = key_grads(key_nope, key_values, key_rope, key_pos)
        key_block, key_rope = passed_along((key_block, key_rope), "ctx", 1)
        latent_acc, rope_acc = (
            passed_along((latent_acc + latent_part).astype(jnp.bfloat16), "ctx", 1).astype(
                jnp.float32
            ),
            passed_along((rope_acc + rope_part).astype(jnp.bfloat16), "ctx", 1).astype(jnp.float32),
        )
        return (key_block, key_rope, latent_acc, rope_acc, query_acc + query_part)

    start_loop = (
        latent,
        rope_key,
        jnp.zeros((rows_dev, D_LAT), jnp.float32),
        jnp.zeros((rows_dev, D_ROPE), jnp.float32),
        zero_query,
    )
    ended = lax.fori_loop(0, ctx_count, visit_block, start_loop)
    latent_acc, rope_acc, query_acc = (ended[2], ended[3], ended[4])
    latent_sum, rope_sum = (
        lax.psum(latent_acc.astype(jnp.bfloat16), "head").astype(jnp.float32),
        lax.psum(rope_acc.astype(jnp.bfloat16), "head").astype(jnp.float32),
    )
    query_grad = query_acc.reshape(rows_dev, head_count * (D_NOPE + D_ROPE)).astype(jnp.bfloat16)
    return (query_grad, latent_sum.astype(jnp.bfloat16), rope_sum.astype(jnp.bfloat16))


def solution(mesh):
    return jax.shard_map(
        on_device,
        mesh=mesh,
        in_specs=(
            P("ctx", "head"),
            P("ctx", None),
            P("ctx", None),
            P(None, "head"),
            P(None, "head"),
            P("head"),
            P("head"),
            P("ctx", "head"),
            P(),
        ),
        out_specs=(P("ctx", "head"), P("ctx", None), P("ctx", None)),
        check_vma=False,
    )
```

profile of v0, /device:TPU:1, one launch (start us, length us, event | category | flops | bytes accessed | tf_op | source)
XLA Modules:
  0.0 504.7 jit_solution(15529020131872376515)
XLA Ops:
  16.4 43.7 %all_gather.7 = bf16[2048,64]{0,1:T(8,128)(2,1)S(1)} all-gather(bf16[128,64]{0,1:T(8,128)(2,1)} %copy.144), channel_id=1, replica_groups=mesh['ctx'=16,'head'=16] {'ctx'}, dimensions={0}, use_global_device_ids=true | all-gather | bytes 278528 | tf_op jit(solution)/shard_map/all_gather | solution.py:148
  61.6 11.0 %all-gather.2.cloned.1.call-done = bf16[2048,512]{1,0:T(8,128)(2,1)} async-done(((bf16[128,512]{1,0:T(8,128)(2,1)}), bf16[2048,512]{1,0:T(8,128)(2,1)}) %all-gather.2.cloned.1.call-update) | async-done | bytes 2097168 | tf_op jit(solution)/shard_map/all_gather | solution.py:147
  82.8 282.5 %while.26 = (s32[]{:T(128)}, bf16[128,512]{1,0:T(8,128)(2,1)S(1)}, bf16[128,64]{0,1:T(8,128)(2,1)}, f32[128,512]{1,0:T(8,128)S(1)}, f32[128,64]{0,1:T(8,128)}, /...) while((s32[]{:T(128)}, bf16[128,512]{1,0:T(8,128)(2,1)S(1)}, ...), condition=%wide.wide.region_11.12_spmd.clone, body=%wide.wide.region_7.11_spmd.clone.sunk | while | flops 379215488 | bytes 12329302 | solution.py:211
  95.5 7.0 %collective-permute-done.3 = bf16[128,64]{0,1:T(8,128)(2,1)S(1)} collective-permute-done((bf16[128,64]{0,1:T(8,128)(2,1)S(1)}, bf16[128,64]{0,1:T(8,128)(2,1)S(1)}, u32[]{:S(2)}, u32[]{:S(2)}) %collective-permute-start.3) | collective-permute-done | bytes 16416 | tf_op jit(solution)/shard_map/while/body/eval_jaxpr/ppermute | solution.py:18
  112.4 7.1 %collective-permute-done.3 = bf16[128,64]{0,1:T(8,128)(2,1)S(1)} collective-permute-done((bf16[128,64]{0,1:T(8,128)(2,1)S(1)}, bf16[128,64]{0,1:T(8,128)(2,1)S(1)}, u32[]{:S(2)}, u32[]{:S(2)}) %collective-permute-start.3) | collective-permute-done | bytes 16416 | tf_op jit(solution)/shard_map/while/body/eval_jaxpr/ppermute | solution.py:18
  128.0 9.0 %collective-permute-done.3 = bf16[128,64]{0,1:T(8,128)(2,1)S(1)} collective-permute-done((bf16[128,64]{0,1:T(8,128)(2,1)S(1)}, bf16[128,64]{0,1:T(8,128)(2,1)S(1)}, u32[]{:S(2)}, u32[]{:S(2)}) %collective-permute-start.3) | collective-permute-done | bytes 16416 | tf_op jit(solution)/shard_map/while/body/eval_jaxpr/ppermute | solution.py:18
  145.2 8.4 %collective-permute-done.3 = bf16[128,64]{0,1:T(8,128)(2,1)S(1)} collective-permute-done((bf16[128,64]{0,1:T(8,128)(2,1)S(1)}, bf16[128,64]{0,1:T(8,128)(2,1)S(1)}, u32[]{:S(2)}, u32[]{:S(2)}) %collective-permute-start.3) | collective-permute-done | bytes 16416 | tf_op jit(solution)/shard_map/while/body/eval_jaxpr/ppermute | solution.py:18
  163.3 7.5 %collective-permute-done.3 = bf16[128,64]{0,1:T(8,128)(2,1)S(1)} collective-permute-done((bf16[128,64]{0,1:T(8,128)(2,1)S(1)}, bf16[128,64]{0,1:T(8,128)(2,1)S(1)}, u32[]{:S(2)}, u32[]{:S(2)}) %collective-permute-start.3) | collective-permute-done | bytes 16416 | tf_op jit(solution)/shard_map/while/body/eval_jaxpr/ppermute | solution.py:18
  178.7 9.0 %collective-permute-done.3 = bf16[128,64]{0,1:T(8,128)(2,1)S(1)} collective-permute-done((bf16[128,64]{0,1:T(8,128)(2,1)S(1)}, bf16[128,64]{0,1:T(8,128)(2,1)S(1)}, u32[]{:S(2)}, u32[]{:S(2)}) %collective-permute-start.3) | collective-permute-done | bytes 16416 | tf_op jit(solution)/shard_map/while/body/eval_jaxpr/ppermute | solution.py:18
  197.1 7.8 %collective-permute-done.3 = bf16[128,64]{0,1:T(8,128)(2,1)S(1)} collective-permute-done((bf16[128,64]{0,1:T(8,128)(2,1)S(1)}, bf16[128,64]{0,1:T(8,128)(2,1)S(1)}, u32[]{:S(2)}, u32[]{:S(2)}) %collective-permute-start.3) | collective-permute-done | bytes 16416 | tf_op jit(solution)/shard_map/while/body/eval_jaxpr/ppermute | solution.py:18
  214.7 6.8 %collective-permute-done.3 = bf16[128,64]{0,1:T(8,128)(2,1)S(1)} collective-permute-done((bf16[128,64]{0,1:T(8,128)(2,1)S(1)}, bf16[128,64]{0,1:T(8,128)(2,1)S(1)}, u32[]{:S(2)}, u32[]{:S(2)}) %collective-permute-start.3) | collective-permute-done | bytes 16416 | tf_op jit(solution)/shard_map/while/body/eval_jaxpr/ppermute | solution.py:18
  232.2 4.0 collective-permute-done.3
  245.3 6.4 %collective-permute-start.3 = (bf16[128,64]{0,1:T(8,128)(2,1)S(1)}, bf16[128,64]{0,1:T(8,128)(2,1)S(1)}, u32[]{:S(2)}, u32[]{:S(2)}) collective-permute-start(bf16[128,64]{0,1:T(8,128)(2,1)S(1)} %fusion.161), channel_id=1, source_target_pairs={{0,16},{16,32},{32,48},{48,64},{64,80},{80,96},{96,112},{112,128},... | collective-permute-start | bytes 49160 | tf_op jit(solution)/shard_map/while/body/eval_jaxpr/ppermute | solution.py:18
  262.0 3.7 collective-permute-start.2
  266.5 5.3 %collective-permute-start.3 = (bf16[128,64]{0,1:T(8,128)(2,1)S(1)}, bf16[128,64]{0,1:T(8,128)(2,1)S(1)}, u32[]{:S(2)}, u32[]{:S(2)}) collective-permute-start(bf16[128,64]{0,1:T(8,128)(2,1)S(1)} %fusion.161), channel_id=1, source_target_pairs={{0,16},{16,32},{32,48},{48,64},{64,80},{80,96},{96,112},{112,128},... | collective-permute-start | bytes 49160 | tf_op jit(solution)/shard_map/while/body/eval_jaxpr/ppermute | solution.py:18
  283.3 4.0 collective-permute-start.3
  287.8 4.8 collective-permute-done.3
  300.0 3.6 collective-permute-start.3
  304.1 4.2 collective-permute-done.3
  320.0 5.8 %collective-permute-done.3 = bf16[128,64]{0,1:T(8,128)(2,1)S(1)} collective-permute-done((bf16[128,64]{0,1:T(8,128)(2,1)S(1)}, bf16[128,64]{0,1:T(8,128)(2,1)S(1)}, u32[]{:S(2)}, u32[]{:S(2)}) %collective-permute-start.3) | collective-permute-done | bytes 16416 | tf_op jit(solution)/shard_map/while/body/eval_jaxpr/ppermute | solution.py:18
  335.4 9.9 %collective-permute-done.3 = bf16[128,64]{0,1:T(8,128)(2,1)S(1)} collective-permute-done((bf16[128,64]{0,1:T(8,128)(2,1)S(1)}, bf16[128,64]{0,1:T(8,128)(2,1)S(1)}, u32[]{:S(2)}, u32[]{:S(2)}) %collective-permute-start.3) | collective-permute-done | bytes 16416 | tf_op jit(solution)/shard_map/while/body/eval_jaxpr/ppermute | solution.py:18
  354.8 9.7 %collective-permute-done.3 = bf16[128,64]{0,1:T(8,128)(2,1)S(1)} collective-permute-done((bf16[128,64]{0,1:T(8,128)(2,1)S(1)}, bf16[128,64]{0,1:T(8,128)(2,1)S(1)}, u32[]{:S(2)}, u32[]{:S(2)}) %collective-permute-start.3) | collective-permute-done | bytes 16416 | tf_op jit(solution)/shard_map/while/body/eval_jaxpr/ppermute | solution.py:18
  367.5 65.2 %psum.15 = bf16[128,64]{0,1:T(8,128)(2,1)} all-reduce(bf16[128,64]{0,1:T(8,128)(2,1)S(1)} %convert_element_type.155), channel_id=1, replica_groups=mesh['ctx'=16,'head'=16] {'head'}, use_global_device_ids=true, to_apply=%region_13.14 | all-reduce | flops 8192 | bytes 32768 | tf_op jit(solution)/shard_map/psum | solution.py:215
  432.7 63.6 %all-reduce.3.cloned.1.call-done = bf16[128,512]{1,0:T(8,128)(2,1)} async-done(((bf16[128,512]{1,0:T(8,128)(2,1)}), bf16[128,512]{1,0:T(8,128)(2,1)}) %all-reduce.3.cloned.1.call-update) | async-done | bytes 131088 | tf_op jit(solution)/shard_map/psum | solution.py:214
  (660 shorter events, 179.5 us)
Async XLA Ops:
  7.2 65.5 %all-gather.2.cloned.1.call-start = ((), (), s32[]{:S(2)}) async-start(), calls=%async_computation | async-start | bytes 2228224 | tf_op jit(solution)/shard_map/all_gather | solution.py:147
  10.2 486.1 %all-reduce.3.cloned.1.call-start = ((), (), s32[]{:S(2)}) async-start(), calls=%async_computation.1 | async-start | bytes 262144 | tf_op jit(solution)/shard_map/psum | solution.py:214
  82.8 20.4 %collective-permute-start = (bf16[128,512]{1,0:T(8,128)(2,1)S(1)}, bf16[128,512]{1,0:T(8,128)(2,1)S(1)}, u32[]{:S(2)}, u32[]{:S(2)}) collective-permute-start(bf16[128,512]{1,0:T(8,128)(2,1)S(1)} %copy.129), channel_id=1, source_target_pairs={{0,16},{16,32},{32,48},{48,64},{64,80},{80,96},{96,112},{112,128},... | collective-permute-start | bytes 393224 | tf_op jit(solution)/shard_map/while/body/eval_jaxpr/ppermute | solution.py:18
  86.0 17.1 %collective-permute-start.1 = (bf16[128,64]{0,1:T(8,128)(2,1)S(1)}, bf16[128,64]{0,1:T(8,128)(2,1)}, u32[]{:S(2)}, u32[]{:S(2)}) collective-permute-start(bf16[128,64]{0,1:T(8,128)(2,1)S(1)} %copy.130), channel_id=1, source_target_pairs={{0,16},{16,32},{32,48},{48,64},{64,80},{80,96},{96,112},{112,128},... | collective-permute-start | bytes 49160 | tf_op jit(solution)/shard_map/while/body/eval_jaxpr/ppermute | solution.py:18
  103.2 16.9 %collective-permute-start = (bf16[128,512]{1,0:T(8,128)(2,1)S(1)}, bf16[128,512]{1,0:T(8,128)(2,1)S(1)}, u32[]{:S(2)}, u32[]{:S(2)}) collective-permute-start(bf16[128,512]{1,0:T(8,128)(2,1)S(1)} %copy.129), channel_id=1, source_target_pairs={{0,16},{16,32},{32,48},{48,64},{64,80},{80,96},{96,112},{112,128},... | collective-permute-start | bytes 393224 | tf_op jit(solution)/shard_map/while/body/eval_jaxpr/ppermute | solution.py:18
  120.2 17.4 %collective-permute-start = (bf16[128,512]{1,0:T(8,128)(2,1)S(1)}, bf16[128,512]{1,0:T(8,128)(2,1)S(1)}, u32[]{:S(2)}, u32[]{:S(2)}) collective-permute-start(bf16[128,512]{1,0:T(8,128)(2,1)S(1)} %copy.129), channel_id=1, source_target_pairs={{0,16},{16,32},{32,48},{48,64},{64,80},{80,96},{96,112},{112,128},... | collective-permute-start | bytes 393224 | tf_op jit(solution)/shard_map/while/body/eval_jaxpr/ppermute | solution.py:18
  121.0 16.6 %collective-permute-start.1 = (bf16[128,64]{0,1:T(8,128)(2,1)S(1)}, bf16[128,64]{0,1:T(8,128)(2,1)}, u32[]{:S(2)}, u32[]{:S(2)}) collective-permute-start(bf16[128,64]{0,1:T(8,128)(2,1)S(1)} %copy.130), channel_id=1, source_target_pairs={{0,16},{16,32},{32,48},{48,64},{64,80},{80,96},{96,112},{112,128},... | collective-permute-start | bytes 49160 | tf_op jit(solution)/shard_map/while/body/eval_jaxpr/ppermute | solution.py:18
  137.7 16.5 %collective-permute-start = (bf16[128,512]{1,0:T(8,128)(2,1)S(1)}, bf16[128,512]{1,0:T(8,128)(2,1)S(1)}, u32[]{:S(2)}, u32[]{:S(2)}) collective-permute-start(bf16[128,512]{1,0:T(8,128)(2,1)S(1)} %copy.129), channel_id=1, source_target_pairs={{0,16},{16,32},{32,48},{48,64},{64,80},{80,96},{96,112},{112,128},... | collective-permute-start | bytes 393224 | tf_op jit(solution)/shard_map/while/body/eval_jaxpr/ppermute | solution.py:18
  154.2 17.3 %collective-permute-start = (bf16[128,512]{1,0:T(8,128)(2,1)S(1)}, bf16[128,512]{1,0:T(8,128)(2,1)S(1)}, u32[]{:S(2)}, u32[]{:S(2)}) collective-permute-start(bf16[128,512]{1,0:T(8,128)(2,1)S(1)} %copy.129), channel_id=1, source_target_pairs={{0,16},{16,32},{32,48},{48,64},{64,80},{80,96},{96,112},{112,128},... | collective-permute-start | bytes 393224 | tf_op jit(solution)/shard_map/while/body/eval_jaxpr/ppermute | solution.py:18
  155.0 16.4 %collective-permute-start.1 = (bf16[128,64]{0,1:T(8,128)(2,1)S(1)}, bf16[128,64]{0,1:T(8,128)(2,1)}, u32[]{:S(2)}, u32[]{:S(2)}) collective-permute-start(bf16[128,64]{0,1:T(8,128)(2,1)S(1)} %copy.130), channel_id=1, source_target_pairs={{0,16},{16,32},{32,48},{48,64},{64,80},{80,96},{96,112},{112,128},... | collective-permute-start | bytes 49160 | tf_op jit(solution)/shard_map/while/body/eval_jaxpr/ppermute | solution.py:18
  171.5 16.8 %collective-permute-start = (bf16[128,512]{1,0:T(8,128)(2,1)S(1)}, bf16[128,512]{1,0:T(8,128)(2,1)S(1)}, u32[]{:S(2)}, u32[]{:S(2)}) collective-permute-start(bf16[128,512]{1,0:T(8,128)(2,1)S(1)} %copy.129), channel_id=1, source_target_pairs={{0,16},{16,32},{32,48},{48,64},{64,80},{80,96},{96,112},{112,128},... | collective-permute-start | bytes 393224 | tf_op jit(solution)/shard_map/while/body/eval_jaxpr/ppermute | solution.py:18
  188.4 17.2 %collective-permute-start = (bf16[128,512]{1,0:T(8,128)(2,1)S(1)}, bf16[128,512]{1,0:T(8,128)(2,1)S(1)}, u32[]{:S(2)}, u32[]{:S(2)}) collective-permute-start(bf16[128,512]{1,0:T(8,128)(2,1)S(1)} %copy.129), channel_id=1, source_target_pairs={{0,16},{16,32},{32,48},{48,64},{64,80},{80,96},{96,112},{112,128},... | collective-permute-start | bytes 393224 | tf_op jit(solution)/shard_map/while/body/eval_jaxpr/ppermute | solution.py:18
  205.7 16.4 %collective-permute-start = (bf16[128,512]{1,0:T(8,128)(2,1)S(1)}, bf16[128,512]{1,0:T(8,128)(2,1)S(1)}, u32[]{:S(2)}, u32[]{:S(2)}) collective-permute-start(bf16[128,512]{1,0:T(8,128)(2,1)S(1)} %copy.129), channel_id=1, source_target_pairs={{0,16},{16,32},{32,48},{48,64},{64,80},{80,96},{96,112},{112,128},... | collective-permute-start | bytes 393224 | tf_op jit(solution)/shard_map/while/body/eval_jaxpr/ppermute | solution.py:18
  236.9 17.0 %collective-permute-start = (bf16[128,512]{1,0:T(8,128)(2,1)S(1)}, bf16[128,512]{1,0:T(8,128)(2,1)S(1)}, u32[]{:S(2)}, u32[]{:S(2)}) collective-permute-start(bf16[128,512]{1,0:T(8,128)(2,1)S(1)} %copy.129), channel_id=1, source_target_pairs={{0,16},{16,32},{32,48},{48,64},{64,80},{80,96},{96,112},{112,128},... | collective-permute-start | bytes 393224 | tf_op jit(solution)/shard_map/while/body/eval_jaxpr/ppermute | solution.py:18
  253.9 20.0 %collective-permute-start = (bf16[128,512]{1,0:T(8,128)(2,1)S(1)}, bf16[128,512]{1,0:T(8,128)(2,1)S(1)}, u32[]{:S(2)}, u32[]{:S(2)}) collective-permute-start(bf16[128,512]{1,0:T(8,128)(2,1)S(1)} %copy.129), channel_id=1, source_target_pairs={{0,16},{16,32},{32,48},{48,64},{64,80},{80,96},{96,112},{112,128},... | collective-permute-start | bytes 393224 | tf_op jit(solution)/shard_map/while/body/eval_jaxpr/ppermute | solution.py:18
  255.8 18.2 %collective-permute-start.1 = (bf16[128,64]{0,1:T(8,128)(2,1)S(1)}, bf16[128,64]{0,1:T(8,128)(2,1)}, u32[]{:S(2)}, u32[]{:S(2)}) collective-permute-start(bf16[128,64]{0,1:T(8,128)(2,1)S(1)} %copy.130), channel_id=1, source_target_pairs={{0,16},{16,32},{32,48},{48,64},{64,80},{80,96},{96,112},{112,128},... | collective-permute-start | bytes 49160 | tf_op jit(solution)/shard_map/while/body/eval_jaxpr/ppermute | solution.py:18
  274.0 19.3 %collective-permute-start = (bf16[128,512]{1,0:T(8,128)(2,1)S(1)}, bf16[128,512]{1,0:T(8,128)(2,1)S(1)}, u32[]{:S(2)}, u32[]{:S(2)}) collective-permute-start(bf16[128,512]{1,0:T(8,128)(2,1)S(1)} %copy.129), channel_id=1, source_target_pairs={{0,16},{16,32},{32,48},{48,64},{64,80},{80,96},{96,112},{112,128},... | collective-permute-start | bytes 393224 | tf_op jit(solution)/shard_map/while/body/eval_jaxpr/ppermute | solution.py:18
  276.4 16.9 %collective-permute-start.1 = (bf16[128,64]{0,1:T(8,128)(2,1)S(1)}, bf16[128,64]{0,1:T(8,128)(2,1)}, u32[]{:S(2)}, u32[]{:S(2)}) collective-permute-start(bf16[128,64]{0,1:T(8,128)(2,1)S(1)} %copy.130), channel_id=1, source_target_pairs={{0,16},{16,32},{32,48},{48,64},{64,80},{80,96},{96,112},{112,128},... | collective-permute-start | bytes 49160 | tf_op jit(solution)/shard_map/while/body/eval_jaxpr/ppermute | solution.py:18
  309.0 17.5 %collective-permute-start = (bf16[128,512]{1,0:T(8,128)(2,1)S(1)}, bf16[128,512]{1,0:T(8,128)(2,1)S(1)}, u32[]{:S(2)}, u32[]{:S(2)}) collective-permute-start(bf16[128,512]{1,0:T(8,128)(2,1)S(1)} %copy.129), channel_id=1, source_target_pairs={{0,16},{16,32},{32,48},{48,64},{64,80},{80,96},{96,112},{112,128},... | collective-permute-start | bytes 393224 | tf_op jit(solution)/shard_map/while/body/eval_jaxpr/ppermute | solution.py:18
  309.8 16.6 %collective-permute-start.1 = (bf16[128,64]{0,1:T(8,128)(2,1)S(1)}, bf16[128,64]{0,1:T(8,128)(2,1)}, u32[]{:S(2)}, u32[]{:S(2)}) collective-permute-start(bf16[128,64]{0,1:T(8,128)(2,1)S(1)} %copy.130), channel_id=1, source_target_pairs={{0,16},{16,32},{32,48},{48,64},{64,80},{80,96},{96,112},{112,128},... | collective-permute-start | bytes 49160 | tf_op jit(solution)/shard_map/while/body/eval_jaxpr/ppermute | solution.py:18
  326.5 19.4 %collective-permute-start = (bf16[128,512]{1,0:T(8,128)(2,1)S(1)}, bf16[128,512]{1,0:T(8,128)(2,1)S(1)}, u32[]{:S(2)}, u32[]{:S(2)}) collective-permute-start(bf16[128,512]{1,0:T(8,128)(2,1)S(1)} %copy.129), channel_id=1, source_target_pairs={{0,16},{16,32},{32,48},{48,64},{64,80},{80,96},{96,112},{112,128},... | collective-permute-start | bytes 393224 | tf_op jit(solution)/shard_map/while/body/eval_jaxpr/ppermute | solution.py:18
  327.3 18.6 %collective-permute-start.1 = (bf16[128,64]{0,1:T(8,128)(2,1)S(1)}, bf16[128,64]{0,1:T(8,128)(2,1)}, u32[]{:S(2)}, u32[]{:S(2)}) collective-permute-start(bf16[128,64]{0,1:T(8,128)(2,1)S(1)} %copy.130), channel_id=1, source_target_pairs={{0,16},{16,32},{32,48},{48,64},{64,80},{80,96},{96,112},{112,128},... | collective-permute-start | bytes 49160 | tf_op jit(solution)/shard_map/while/body/eval_jaxpr/ppermute | solution.py:18
  346.0 19.2 %collective-permute-start = (bf16[128,512]{1,0:T(8,128)(2,1)S(1)}, bf16[128,512]{1,0:T(8,128)(2,1)S(1)}, u32[]{:S(2)}, u32[]{:S(2)}) collective-permute-start(bf16[128,512]{1,0:T(8,128)(2,1)S(1)} %copy.129), channel_id=1, source_target_pairs={{0,16},{16,32},{32,48},{48,64},{64,80},{80,96},{96,112},{112,128},... | collective-permute-start | bytes 393224 | tf_op jit(solution)/shard_map/while/body/eval_jaxpr/ppermute | solution.py:18
  346.8 18.4 %collective-permute-start.1 = (bf16[128,64]{0,1:T(8,128)(2,1)S(1)}, bf16[128,64]{0,1:T(8,128)(2,1)}, u32[]{:S(2)}, u32[]{:S(2)}) collective-permute-start(bf16[128,64]{0,1:T(8,128)(2,1)S(1)} %copy.130), channel_id=1, source_target_pairs={{0,16},{16,32},{32,48},{48,64},{64,80},{80,96},{96,112},{112,128},... | collective-permute-start | bytes 49160 | tf_op jit(solution)/shard_map/while/body/eval_jaxpr/ppermute | solution.py:18
  (79 other events, 826.1 us)
Sparse Core Ops, SparseCore 0:
  11.0 61.5 all-gather.1
  366.0 130.2 all-reduce.2
where the time goes:
time: 508 us; the launch traced here: 505 us
  waiting for transfers between devices  178 us (35%)
  blocking collectives  109 us (21%)
  matrix products  58.2 us (11%)
  starting transfers between devices  57.4 us (11%)
  other arithmetic  56.3 us (11%)
  local copies, waits for them, and re-layouts  28.4 us (6%)
  between operations  14.2 us (3%)
    ppermute x64, waiting for transfers between devices, passed_along(): return lax.ppermute(value, axis, pairs)  103 us
    psum x1, blocking collectives, on_device(): lax.psum(rope_acc.astype(jnp.bfloat16), 'head').astype(jnp.float32)  65.2 us
    psum x1, waiting for transfers between devices, on_device(): lax.psum(latent_acc.astype(jnp.bfloat16), 'head').astype(jnp.float32)  63.6 us
    ppermute x64, starting transfers between devices, passed_along(): return lax.ppermute(value, axis, pairs)  57.3 us
    all_gather x1, blocking collectives, on_device(): key_rope = lax.all_gather(rope_key, 'ctx', axis=0, tiled=True)  43.7 us
    dot_general x17, matrix products, score_tile(): jnp.einsum('ihd,khd->hik', query_heads[:, :, :D_NOPE], key_nope, preferre...  16.5 us
    while x112, local copies, waits for them, and re-layouts  14.5 us
    reduce_sum x18, other arithmetic, slot_positions(): jnp.sum(jnp.where(table, block_order[None, :], 0), axis=1) * half_rows  13.4 us
  transfers between devices with their start and end apart: 66, of which 18 were waited for; matrix products, arithmetic and copies ran while one was open for 25% of the time, Pallas kernels for 0%

commit v1 on v0

v1 whole, which is shorter than its diff:
```python
import functools

import jax
import jax.numpy as jnp
from jax import lax
from jax.experimental import pallas as pl
from jax.experimental.pallas import tpu as pltpu
from jax.sharding import PartitionSpec as P

MESH = pl.DeviceIdType.MESH
D_LAT = 512
D_NOPE = 128
D_ROPE = 64
D_QK = D_NOPE + D_ROPE
PAIR_WIDTH = 256
ROWS = 128
WIDE = 640
HALF = 64
CHUNKS = 8
CHUNK = 256
PIECE = 16
MAPS = 4
PAIRS_DEV = 2
LOGIT_SCALE = D_QK**-0.5
LOG2E = 1.4426950408889634
EPS = 1e-6
F32 = jnp.float32
BF16 = jnp.bfloat16


class Place:
    def __init__(self):
        ctx, head = lax.axis_index("ctx"), lax.axis_index("head")
        self.x, self.zh = lax.rem(ctx, 4), lax.div(ctx, 4)
        self.y = lax.div(head, 4)
        self.zl = lax.rem(lax.div(head, 2), 2)
        self.c = lax.rem(head, 2)
        self.o = 1 - self.c
        self.first = self.y * self.o + self.x * self.c
        self.last = self.x * self.o + self.y * self.c

    def at(self, x=None, y=None, zh=None, zl=None, c=None):
        x = self.x if x is None else x
        y = self.y if y is None else y
        zh = self.zh if zh is None else zh
        zl = self.zl if zl is None else zl
        c = self.c if c is None else c
        return (zh * 4 + x, y * 4 + zl * 2 + c)

    def first_peer(self, d):
        return self.at(x=lax.rem(self.x + d * self.c, 4), y=lax.rem(self.y + d * self.o, 4))

    def last_peer(self, d):
        return self.at(x=lax.rem(self.x + d * self.o, 4), y=lax.rem(self.y + d * self.c, 4))

    def sibling(self):
        return self.at(c=self.o)


def remote(src, dst, send, recv, device):
    return pltpu.make_async_remote_copy(
        src_ref=src, dst_ref=dst, send_sem=send, recv_sem=recv, device_id=device, device_id_type=MESH
    )


def greet(devices, count):
    barrier = pltpu.get_barrier_semaphore()
    for device in devices:
        pl.semaphore_signal(barrier, inc=1, device_id=device, device_id_type=MESH)
    pl.semaphore_wait(barrier, count)


def gather_kernel(latent, rope, out, z_send, z_recv, f_send, f_recv, l_send, l_recv, s_send, s_recv):
    me = Place()
    base = me.c * 4
    row = pl.multiple_of(me.c * HALF + me.y * PIECE, PIECE)
    mine = out.at[base + me.last]
    mine[me.zh, me.first, :, 0:D_LAT] = latent[pl.ds(row, PIECE), :]
    mine[me.zh, me.first, :, D_LAT:WIDE] = jnp.concatenate(
        [rope[pl.ds(row, PIECE), :], jnp.zeros((PIECE, D_ROPE), BF16)], axis=1
    )
    step = 2 * me.zl - 1
    ahead = lax.rem(me.zh + step + 4, 4)
    behind = lax.rem(me.zh - step + 4, 4)
    across = lax.rem(me.zh + 2, 4)
    z_to = [me.at(zh=ahead, zl=0), me.at(zh=ahead, zl=1), me.at(zh=across, zl=1 - me.zl)]
    z_from = [
        me.at(zh=lax.rem(me.zh + 3, 4), zl=1),
        me.at(zh=lax.rem(me.zh + 1, 4), zl=0),
        me.at(zh=across, zl=1 - me.zl),
    ]
    firsts = [me.first_peer(d) for d in (1, 2, 3)]
    lasts = [me.last_peer(d) for d in (1, 2, 3)]
    greet(z_from + firsts + lasts + [me.sibling()], 10)

    sent = []
    for i, device in enumerate(z_to):
        piece = mine.at[me.zh, me.first]
        copy = remote(piece, piece, z_send.at[i], z_recv.at[me.zh], device)
        copy.start()
        sent.append(copy)
    for d in (1, 2, 3):
        other = lax.rem(me.zh + d, 4)
        piece = mine.at[other, me.first]
        remote(piece, piece, z_send.at[0], z_recv.at[other], z_to[0]).wait_recv()
    for i, device in enumerate(firsts):
        piece = mine.at[:, me.first]
        copy = remote(piece, piece, f_send.at[i], f_recv.at[me.first], device)
        copy.start()
        sent.append(copy)
    for d in (1, 2, 3):
        other = lax.rem(me.first + d, 4)
        piece = mine.at[:, other]
        remote(piece, piece, f_send.at[0], f_recv.at[other], firsts[0]).wait_recv()
    for i, device in enumerate(lasts):
        copy = remote(mine, mine, l_send.at[i], l_recv.at[me.last], device)
        copy.start()
        sent.append(copy)
    for d in (0, 1, 3, 2):
        other = lax.rem(me.last + d, 4)
        piece = out.at[base + other]
        if d:
            remote(piece, piece, l_send.at[0], l_recv.at[other], lasts[0]).wait_recv()
        copy = remote(piece, piece, s_send.at[d], s_recv.at[other], me.sibling())
        copy.start()
        sent.append(copy)
    for d in range(4):
        piece = out.at[me.o * 4 + d]
        remote(piece, piece, s_send.at[0], s_recv.at[d], me.sibling()).wait_recv()
    for copy in sent:
        copy.wait_send()


def total_of(parts):
    total = parts[0].astype(F32)
    for part in parts[1:]:
        total = total + part.astype(F32)
    return total


def scatter_kernel(
    part, latent_out, rope_out,
    from_s, own, from_l, middle, from_f, small, from_z, result,
    s_send, s_recv, l_send, l_recv, f_send, f_recv, z_send, z_recv, e_send, e_recv,
):
    me = Place()
    base = me.c * 4
    firsts = [me.first_peer(d) for d in (1, 2, 3)]
    lasts = [me.last_peer(d) for d in (1, 2, 3)]
    zs = []
    for d in range(1, 8):
        z = lax.rem(me.zh * 2 + me.zl + d, 8)
        zs.append((lax.div(z, 2), lax.rem(z, 2)))
    z_devices = [me.at(zh=zh, zl=zl) for zh, zl in zs]
    others = [me.at(y=lax.rem(me.y + d, 4), c=c) for d in (1, 2, 3) for c in (0, 1)]
    x_line = [me.at(x=lax.rem(me.x + d, 4)) for d in (1, 2, 3)]
    greet(x_line + others + z_devices + [me.sibling()], 17)

    sent = []
    for d in (1, 3, 2, 0):
        chunk = lax.rem(me.first + d, 4)
        copy = remote(
            part.at[me.o * 4 + chunk], from_s.at[chunk], s_send.at[d], s_recv.at[chunk], me.sibling()
        )
        copy.start()
        sent.append(copy)
    for d in (1, 3, 2, 0):
        chunk = lax.rem(me.last + d, 4)
        there = from_s.at[chunk]
        remote(there, there, s_send.at[0], s_recv.at[chunk], me.sibling()).wait_recv()
        own[chunk] = total_of([part[base + chunk], from_s[chunk]]).astype(BF16)
        if d:
            copy = remote(own.at[chunk], from_l.at[d - 1], l_send.at[d - 1], l_recv.at[d - 1], lasts[d - 1])
            copy.start()
            sent.append(copy)
    for d in range(3):
        there = from_l.at[d]
        remote(there, there, l_send.at[0], l_recv.at[d], lasts[0]).wait_recv()
    middle[...] = total_of([own[me.last], from_l[0], from_l[1], from_l[2]]).astype(BF16)
    for d in (1, 2, 3):
        other = lax.rem(me.first + d, 4)
        copy = remote(
            middle.at[:, other], from_f.at[d - 1], f_send.at[d - 1], f_recv.at[d - 1], firsts[d - 1]
        )
        copy.start()
        sent.append(copy)
    for d in range(3):
        there = from_f.at[d]
        remote(there, there, f_send.at[0], f_recv.at[d], firsts[0]).wait_recv()
    small[...] = total_of([middle[:, me.first], from_f[0], from_f[1], from_f[2]]).astype(BF16)
    z_mine = me.zh * 2 + me.zl
    for i, (zh, zl) in enumerate(zs):
        copy = remote(small.at[zh], from_z.at[z_mine], z_send.at[i], z_recv.at[z_mine], z_devices[i])
        copy.start()
        sent.append(copy)
    from_z[z_mine] = small[me.zh]
    for d in range(1, 8):
        z = lax.rem(z_mine + d, 8)
        there = from_z.at[z]
        remote(there, there, z_send.at[0], z_recv.at[z], z_devices[0]).wait_recv()
    place = me.c * 4 + me.y
    result[place] = total_of([from_z[z] for z in range(8)]).astype(BF16)
    ends = others + [me.sibling()]
    for i, device in enumerate(ends):
        copy = remote(result.at[place], result.at[place], e_send.at[i], e_recv.at[place], device)
        copy.start()
        sent.append(copy)
    for d in range(1, 8):
        other = lax.rem(place + d, 8)
        there = result.at[other]
        remote(there, there, e_send.at[0], e_recv.at[other], ends[0]).wait_recv()
    for i in range(8):
        latent_out[i * PIECE : (i + 1) * PIECE, :] = result[i, :, 0:D_LAT]
        rope_out[i * PIECE : (i + 1) * PIECE, :] = result[i, :, D_LAT : D_LAT + D_ROPE]
    for copy in sent:
        copy.wait_send()


NT = (((1,), (1,)), ((), ()))
TN = (((0,), (0,)), ((), ()))


def dot(a, b, dims=None):
    if dims is None:
        return jnp.dot(a, b, preferred_element_type=F32)
    return lax.dot_general(a, b, dims, preferred_element_type=F32)


def compute_kernel(
    lam, queries, keys, key_weight, value_weight, gain, out_grad, query_pos, key_pos,
    query_grad, part,
    q_cat, k_cat, values, scores, tops, outs, totals, lowered, deltas, q_acc,
):
    for h in range(MAPS):
        q_cat[h] = jnp.concatenate(
            [queries[:, h * D_QK : (h + 1) * D_QK], jnp.zeros((ROWS, 256 - D_QK), BF16)], axis=1
        )
    tops[...] = jnp.full(tops.shape, -jnp.inf, F32)
    outs[...] = jnp.zeros(outs.shape, F32)
    totals[...] = jnp.zeros(totals.shape, F32)
    q_acc[...] = jnp.zeros(q_acc.shape, F32)

    def expand(i, carry):
        latent = keys[i, :, 0:D_LAT]
        rope = keys[i, :, D_LAT:WIDE]
        nope = dot(latent, key_weight[...]).astype(BF16)
        value = dot(latent, value_weight[...]).astype(BF16)
        seen = key_pos[i] <= query_pos[...]
        for p in range(PAIRS_DEV):
            values[i, p] = value[:, p * PAIR_WIDTH : (p + 1) * PAIR_WIDTH]
        for h in range(MAPS):
            k_cat[i, h, :, 0:D_NOPE] = nope[:, h * D_NOPE : (h + 1) * D_NOPE]
            k_cat[i, h, :, D_NOPE:256] = rope
            tile = jnp.where(seen, dot(q_cat[h], k_cat[i, h], NT), -jnp.inf)
            scores[i, h] = tile
            tops[h] = jnp.maximum(tops[h], jnp.maximum(tile[:, 0:128], tile[:, 128:256]))
        return carry

    lax.fori_loop(0, CHUNKS, expand, 0)

    for h in range(MAPS):
        tops[h] = jnp.broadcast_to(jnp.max(tops[h], axis=1, keepdims=True), (ROWS, 128))

    def forward(i, carry):
        for p in range(PAIRS_DEV):
            both = []
            for m in range(2):
                h = 2 * p + m
                top = jnp.concatenate([tops[h], tops[h]], axis=1)
                weight = jnp.exp2((scores[i, h] - top) * (LOGIT_SCALE * LOG2E))
                scores[i, h] = weight
                totals[h] += weight[:, 0:128] + weight[:, 128:256]
                both.append(weight.astype(BF16))
            outs[p] += dot(jnp.concatenate(both, axis=0), values[i, p])
        return carry

    lax.fori_loop(0, CHUNKS, forward, 0)

    for p in range(PAIRS_DEV):
        lam_p = lam[p]
        maps = []
        for m in range(2):
            h = 2 * p + m
            inverse = 1.0 / jnp.sum(totals[h], axis=1, keepdims=True)
            totals[h] = jnp.broadcast_to(inverse, (ROWS, 128))
            maps.append(outs[p, m * ROWS : (m + 1) * ROWS] * inverse)
        mixed = maps[0] - lam_p * maps[1]
        inv_root = lax.rsqrt(jnp.mean(mixed * mixed, axis=1, keepdims=True) + EPS)
        normed = mixed * inv_root
        scaled = out_grad[:, p * PAIR_WIDTH : (p + 1) * PAIR_WIDTH].astype(F32) * gain[
            :, p * PAIR_WIDTH : (p + 1) * PAIR_WIDTH
        ]
        d_mixed = (scaled - normed * jnp.mean(scaled * normed, axis=1, keepdims=True)) * inv_root
        lowered[p] = d_mixed.astype(BF16)
        deltas[2 * p] = jnp.broadcast_to(
            jnp.sum(d_mixed * maps[0], axis=1, keepdims=True), (ROWS, 128)
        )
        deltas[2 * p + 1] = jnp.broadcast_to(
            -lam_p * jnp.sum(d_mixed * maps[1], axis=1, keepdims=True), (ROWS, 128)
        )

    def backward(i, carry):
        d_nope = []
        d_value = []
        d_rope = jnp.zeros((CHUNK, 128), F32)
        for p in range(PAIRS_DEV):
            lam_p = lam[p]
            grad = lowered[p]
            through = dot(grad, values[i, p], NT)
            probs = []
            for m in range(2):
                h = 2 * p + m
                probs.append(scores[i, h] * jnp.concatenate([totals[h], totals[h]], axis=1))
            d_value.append(dot((probs[0] - lam_p * probs[1]).astype(BF16), grad, TN).astype(BF16))
            for m in range(2):
                h = 2 * p + m
                delta = jnp.concatenate([deltas[h], deltas[h]], axis=1)
                inner = through if m == 0 else -lam_p * through
                d_score = (probs[m] * (inner - delta)).astype(BF16)
                q_acc[h] += dot(d_score, k_cat[i, h])
                d_key = dot(d_score, q_cat[h], TN) * LOGIT_SCALE
                d_nope.append(d_key[:, 0:D_NOPE].astype(BF16))
                d_rope = d_rope + d_key[:, D_NOPE:256]
        d_latent = dot(jnp.concatenate(d_nope, axis=1), key_weight[...], NT)
        d_latent = d_latent + dot(jnp.concatenate(d_value, axis=1), value_weight[...], NT)
        part[i, :, 0:D_LAT] = d_latent.astype(BF16)
        part[i, :, D_LAT:WIDE] = d_rope.astype(BF16)
        return carry

    lax.fori_loop(0, CHUNKS, backward, 0)
    for h in range(MAPS):
        query_grad[:, h * D_QK : (h + 1) * D_QK] = (q_acc[h, :, 0:D_QK] * LOGIT_SCALE).astype(BF16)


VMEM = pl.BlockSpec(memory_space=pltpu.VMEM)
SMEM = pl.BlockSpec(memory_space=pltpu.SMEM)
DMA = pltpu.SemaphoreType.DMA


def gather_keys(latent, rope_key):
    return pl.pallas_call(
        gather_kernel,
        out_shape=jax.ShapeDtypeStruct((CHUNKS, 4, 4, PIECE, WIDE), BF16),
        in_specs=[VMEM, VMEM],
        out_specs=VMEM,
        scratch_shapes=[DMA((n,)) for n in (3, 4, 3, 4, 3, 4, 4, 4)],
        compiler_params=pltpu.CompilerParams(
            collective_id=0, has_side_effects=True, vmem_limit_bytes=32 << 20
        ),
        name="gather_keys",
    )(latent, rope_key)


def scatter_grads(part):
    chunk = (4, 4, PIECE, WIDE)
    return pl.pallas_call(
        scatter_kernel,
        out_shape=(
            jax.ShapeDtypeStruct((ROWS, D_LAT), BF16),
            jax.ShapeDtypeStruct((ROWS, D_ROPE), BF16),
        ),
        in_specs=[VMEM],
        out_specs=(VMEM, VMEM),
        scratch_shapes=[
            pltpu.VMEM((4,) + chunk, BF16),
            pltpu.VMEM((4,) + chunk, BF16),
            pltpu.VMEM((3,) + chunk, BF16),
            pltpu.VMEM(chunk, BF16),
            pltpu.VMEM((3, 4, PIECE, WIDE), BF16),
            pltpu.VMEM((4, PIECE, WIDE), BF16),
            pltpu.VMEM((8, PIECE, WIDE), BF16),
            pltpu.VMEM((8, PIECE, WIDE), BF16),
        ]
        + [DMA((n,)) for n in (4, 4, 3, 3, 3, 3, 7, 8, 7, 8)],
        compiler_params=pltpu.CompilerParams(
            collective_id=1, has_side_effects=True, vmem_limit_bytes=32 << 20
        ),
        name="scatter_grads",
    )(part)


def attend(lam, queries, keys, key_weight, value_weight, gain, out_grad, query_pos, key_pos):
    return pl.pallas_call(
        compute_kernel,
        out_shape=(
            jax.ShapeDtypeStruct((ROWS, MAPS * D_QK), BF16),
            jax.ShapeDtypeStruct((CHUNKS, CHUNK, WIDE), BF16),
        ),
        in_specs=[SMEM] + [VMEM] * 8,
        out_specs=(VMEM, VMEM),
        scratch_shapes=[
            pltpu.VMEM((MAPS, ROWS, 256), BF16),
            pltpu.VMEM((CHUNKS, MAPS, CHUNK, 256), BF16),
            pltpu.VMEM((CHUNKS, PAIRS_DEV, CHUNK, PAIR_WIDTH), BF16),
            pltpu.VMEM((CHUNKS, MAPS, ROWS, CHUNK), F32),
            pltpu.VMEM((MAPS, ROWS, 128), F32),
            pltpu.VMEM((PAIRS_DEV, 2 * ROWS, PAIR_WIDTH), F32),
            pltpu.VMEM((MAPS, ROWS, 128), F32),
            pltpu.VMEM((PAIRS_DEV, ROWS, PAIR_WIDTH), BF16),
            pltpu.VMEM((MAPS, ROWS, 128), F32),
            pltpu.VMEM((MAPS, ROWS, 256), F32),
        ],
        compiler_params=pltpu.CompilerParams(vmem_limit_bytes=48 << 20),
        name="attend",
    )(lam, queries, keys, key_weight, value_weight, gain, out_grad, query_pos, key_pos)


def key_tokens():
    last = jnp.arange(4)[:, None, None, None]
    z = jnp.arange(4)[None, :, None, None]
    first = jnp.arange(4)[None, None, :, None]
    r = jnp.arange(PIECE)[None, None, None, :]
    zero = (z * 4 + last) * ROWS + first * PIECE + r
    one = (z * 4 + first) * ROWS + HALF + last * PIECE + r
    return jnp.stack([zero, one]).astype(jnp.int32)


def on_device(
    queries, latent, rope_key, key_weight, value_weight, lambda_pair, norm_gain, out_grad, block_order
):
    me = lax.axis_index("ctx")
    tokens = key_tokens()
    slots = (tokens[..., 0] // HALF).reshape(-1)
    hot = slots[:, None] == jnp.arange(32, dtype=jnp.int32)[None, :]
    blocks = jnp.sum(jnp.where(hot, block_order[None, :], 0), axis=1)
    key_pos = (blocks[:, None] * HALF + (tokens % HALF).reshape(-1, PIECE)).reshape(CHUNKS, 1, CHUNK)
    my_slots = jnp.arange(2, dtype=jnp.int32) + 2 * me
    hot = my_slots[:, None] == jnp.arange(32, dtype=jnp.int32)[None, :]
    mine = jnp.sum(jnp.where(hot, block_order[None, :], 0), axis=1)
    query_pos = (mine[:, None] * HALF + jnp.arange(HALF, dtype=jnp.int32)[None, :]).reshape(ROWS, 1)

    keys = gather_keys(latent, rope_key).reshape(CHUNKS, CHUNK, WIDE)
    query_grad, part = attend(
        lambda_pair, queries, keys, key_weight, value_weight, norm_gain.reshape(1, -1), out_grad,
        query_pos, key_pos,
    )
    latent_grad, rope_grad = scatter_grads(part.reshape(CHUNKS, 4, 4, PIECE, WIDE))
    return (query_grad, latent_grad, rope_grad)


def solution(mesh):
    return jax.shard_map(
        on_device,
        mesh=mesh,
        in_specs=(
            P("ctx", "head"),
            P("ctx", None),
            P("ctx", None),
            P(None, "head"),
            P(None, "head"),
            P("head"),
            P("head"),
            P("ctx", "head"),
            P(),
        ),
        out_specs=(P("ctx", "head"), P("ctx", None), P("ctx", None)),
        check_vma=False,
    )
```

time: 508 us -> 93.7 us (0.18)
  waiting for transfers between devices: 178 us -> 0 us
  blocking collectives: 109 us -> 0 us
  Pallas kernels: 0 us -> 84.8 us
  matrix products: 58.2 us -> 0 us
  starting transfers between devices: 57.4 us -> 0 us
  other arithmetic: 56.3 us -> 2.72 us
  local copies, waits for them, and re-layouts: 28.4 us -> 5.21 us
  between operations: 14.2 us -> 0.77 us
    ppermute x64 -> x0, waiting for transfers between devices: 103 us -> none  [passed_along(): return lax.ppermute(value, axis, pairs)]
    pallas_call x0 -> x3, Pallas kernels: none -> 84.8 us  [the longest x1 35.1 us: scatter_grads(): pl.pallas_call(scatter_kernel, out_shape=(jax.ShapeDtypeStruct((ROWS, D_L...]
    psum x1 -> x0, blocking collectives: 65.2 us -> none  [on_device(): lax.psum(rope_acc.astype(jnp.bfloat16), 'head').astype(jnp.float32)]
    psum x1 -> x0, waiting for transfers between devices: 63.6 us -> none  [on_device(): lax.psum(latent_acc.astype(jnp.bfloat16), 'head').astype(jnp.float32)]
    dot_general x181 -> x0, matrix products: 58.2 us -> none  [the longest x17 16.5 us: score_tile(): jnp.einsum('ihd,khd->hik', query_heads[:, :, :D_NOPE], key_nope, preferre...]
    ppermute x64 -> x0, starting transfers between devices: 57.3 us -> none  [passed_along(): return lax.ppermute(value, axis, pairs)]
    all_gather x1 -> x0, blocking collectives: 43.7 us -> none  [on_device(): key_rope = lax.all_gather(rope_key, 'ctx', axis=0, tiled=True)]
    convert_element_type x53 -> x0, other arithmetic: 23.9 us -> none  [the longest x16 11.6 us: visit_block(): (rope_acc + rope_part).astype(jnp.bfloat16)]
  transfers between devices with their start and end apart: 66 -> 0, of which waited for: 18 -> 0; matrix products, arithmetic and copies ran while one was open for 25% -> 0% of each run, Pallas kernels for 0% -> 0%
where the time goes in v1:
time: 93.7 us; the launch traced here: 93.5 us
  Pallas kernels  84.8 us (91%)
  local copies, waits for them, and re-layouts  5.21 us (6%)
  other arithmetic  2.72 us (3%)
    pallas_call x1, Pallas kernels, scatter_grads(): pl.pallas_call(scatter_kernel, out_shape=(jax.ShapeDtypeStruct((ROWS, D_L...  35.1 us
    pallas_call x1, Pallas kernels, gather_keys(): pl.pallas_call(gather_kernel, out_shape=jax.ShapeDtypeStruct((CHUNKS, 4,...  31.7 us
    pallas_call x1, Pallas kernels, attend(): pl.pallas_call(compute_kernel, out_shape=(jax.ShapeDtypeStruct((ROWS, MAP...  17.9 us
    unnamed x19, local copies, waits for them, and re-layouts  4.59 us

profile of v1, /device:TPU:1, one launch (start us, length us, event | category | flops | bytes accessed | tf_op | source)
XLA Modules:
  0.0 93.5 jit_solution(9393082992595762339)
XLA Ops:
  0.6 0.0 copy-start.2
  0.6 0.0 copy-start.1
  0.7 0.9 fusion.4
  1.6 0.1 iota_add_fusion.2
  1.7 0.1 multiply_add_fusion
  1.8 0.1 broadcast_add_fusion
  1.8 0.8 copy.22.rope
  2.7 0.1 iota_add_fusion
  2.8 0.6 fusion.1
  3.4 0.1 squeeze.3
  3.6 0.7 select_reduce_fusion
  4.3 0.1 stack.8
  4.4 0.1 mul.73
  4.5 0.1 add.214
  4.6 0.1 add.215
  4.7 0.1 add.218.query_pos
  4.9 0.0 copy-start.4
  4.9 0.9 copy-done.4
  5.8 31.7 %gather_keys.1 = bf16[8,4,4,16,640]{4,3,2,1,0:T(8,128)(2,1)S(1)} custom-call(bf16[128,512]{1,0:T(8,128)(2,1)S(1)} %copy-done.4, bf16[128,64]{1,0:T(8,128)(2,1)S(1)} %copy.22.rope), custom_call_target="tpu_custom_call" | custom-call | tf_op jit(solution)/shard_map/gather_keys/pallas_call | solution.py:341
  37.5 1.5 %copy-done = bf16[8,4,4,16,640]{4,3,2,1,0:T(8,128)(2,1)} copy-done((bf16[8,4,4,16,640]{4,3,2,1,0:T(8,128)(2,1)}, bf16[8,4,4,16,640]{4,3,2,1,0:T(8,128)(2,1)S(1)}, u32[]{:S(2)}) %copy-start) | copy-done | bytes 2621464
  39.0 17.9 %attend.1 = (bf16[128,768]{1,0:T(8,128)(2,1)}, bf16[8,256,640]{2,1,0:T(8,128)(2,1)S(1)}) custom-call(f32[2]{0:T(128)S(1)} %copy-done.7, bf16[128,768]{1,0:T(8,128)(2,1)S(1)} %copy-done.3, bf16[8,256,640]{2,1,0:T(8,128)(2,1)} %bitcast.3, bf16[512,512]{1,0:T(8,128)(2,1)S(1)} %copy-done.1, bf16[512,512]{1,0:T(8,128)(2,1)S(1)} %copy-done.2, ...), custom_call_target="tpu_custom_call" | custom-call | tf_op jit(solution)/shard_map/attend/pallas_call | solution.py:383
  57.0 35.1 %scatter_grads.1 = (bf16[128,512]{1,0:T(8,128)(2,1)S(1)}, bf16[128,64]{1,0:T(8,128)(2,1)S(1)}) custom-call(bf16[8,4,4,16,640]{4,3,2,1,0:T(8,128)(2,1)S(1)} %bitcast.4), custom_call_target="tpu_custom_call" | custom-call | tf_op jit(solution)/shard_map/scatter_grads/pallas_call | solution.py:356
  92.1 0.7 copy.24
  92.8 0.7 copy.26
  (19 shorter events, 0.1 us)
Async XLA Ops:
  0.6 38.4 %copy-start.2 = (bf16[512,512]{1,0:T(8,128)(2,1)S(1)}, bf16[512,512]{1,0:T(8,128)(2,1)}, u32[]{:S(2)}) copy-start(bf16[512,512]{1,0:T(8,128)(2,1)} %value_weight.1) | copy-start | bytes 1572868
  0.6 38.4 %copy-start.1 = (bf16[512,512]{1,0:T(8,128)(2,1)S(1)}, bf16[512,512]{1,0:T(8,128)(2,1)}, u32[]{:S(2)}) copy-start(bf16[512,512]{1,0:T(8,128)(2,1)} %key_weight.1) | copy-start | bytes 1572868
  0.7 38.4 %copy-start.3 = (bf16[128,768]{1,0:T(8,128)(2,1)S(1)}, bf16[128,768]{1,0:T(8,128)(2,1)}, u32[]{:S(2)}) copy-start(bf16[128,768]{1,0:T(8,128)(2,1)} %queries.1) | copy-start | bytes 589828
  4.9 0.9 copy-start.4
  5.8 33.2 %copy-start.5 = (bf16[128,512]{1,0:T(8,128)(2,1)S(1)}, bf16[128,512]{1,0:T(8,128)(2,1)}, u32[]{:S(2)}) copy-start(bf16[128,512]{1,0:T(8,128)(2,1)} %out_grad.1) | copy-start | bytes 393220
  5.8 33.2 %copy-start.6 = (f32[512]{0:T(512)S(1)}, f32[512]{0:T(512)}, u32[]{:S(2)}) copy-start(f32[512]{0:T(512)} %param.15) | copy-start | bytes 6148
  5.8 33.2 %copy-start.7 = (f32[2]{0:T(128)S(1)}, f32[2]{0:T(128)}, u32[]{:S(2)}) copy-start(f32[2]{0:T(128)} %lam.1) | copy-start | bytes 28
  37.5 1.5 %copy-start = (bf16[8,4,4,16,640]{4,3,2,1,0:T(8,128)(2,1)}, bf16[8,4,4,16,640]{4,3,2,1,0:T(8,128)(2,1)S(1)}, u32[]{:S(2)}) copy-start(bf16[8,4,4,16,640]{4,3,2,1,0:T(8,128)(2,1)S(1)} %gather_keys.1) | copy-start | bytes 7864324

commit v2 on v1

v2 whole, which is shorter than its diff:
```python
import functools

import jax
import jax.numpy as jnp
from jax import lax
from jax.experimental import pallas as pl
from jax.experimental.pallas import tpu as pltpu
from jax.sharding import PartitionSpec as P

MESH = pl.DeviceIdType.MESH
D_LAT = 512
D_NOPE = 128
D_ROPE = 64
D_QK = D_NOPE + D_ROPE
PAIR_WIDTH = 256
ROWS = 128
WIDE = 640
HALF = 64
CHUNKS = 8
CHUNK = 256
PIECE = 16
MAPS = 4
PAIRS_DEV = 2
LOGIT_SCALE = D_QK**-0.5
LOG2E = 1.4426950408889634
EPS = 1e-6
F32 = jnp.float32
BF16 = jnp.bfloat16


class Place:
    def __init__(self):
        ctx, head = lax.axis_index("ctx"), lax.axis_index("head")
        self.x, self.zh = lax.rem(ctx, 4), lax.div(ctx, 4)
        self.y = lax.div(head, 4)
        self.zl = lax.rem(lax.div(head, 2), 2)
        self.c = lax.rem(head, 2)
        self.o = 1 - self.c
        self.first = self.y * self.o + self.x * self.c
        self.last = self.x * self.o + self.y * self.c

    def at(self, x=None, y=None, zh=None, zl=None, c=None):
        x = self.x if x is None else x
        y = self.y if y is None else y
        zh = self.zh if zh is None else zh
        zl = self.zl if zl is None else zl
        c = self.c if c is None else c
        return (zh * 4 + x, y * 4 + zl * 2 + c)

    def first_peer(self, d):
        return self.at(x=lax.rem(self.x + d * self.c, 4), y=lax.rem(self.y + d * self.o, 4))

    def last_peer(self, d):
        return self.at(x=lax.rem(self.x + d * self.o, 4), y=lax.rem(self.y + d * self.c, 4))

    def z_peer(self, d):
        z = lax.rem(self.zh * 2 + self.zl + d, 8)
        return self.at(zh=lax.div(z, 2), zl=lax.rem(z, 2))

    def sibling(self):
        return self.at(c=self.o)


def remote(src, dst, send, recv, device):
    return pltpu.make_async_remote_copy(
        src_ref=src, dst_ref=dst, send_sem=send, recv_sem=recv, device_id=device, device_id_type=MESH
    )


def greet(devices, count):
    barrier = pltpu.get_barrier_semaphore()
    for device in devices:
        pl.semaphore_signal(barrier, inc=1, device_id=device, device_id_type=MESH)
    pl.semaphore_wait(barrier, count)


NT = (((1,), (1,)), ((), ()))
TN = (((0,), (0,)), ((), ()))


def dot(a, b, dims=None):
    if dims is None:
        return jnp.dot(a, b, preferred_element_type=F32)
    return lax.dot_general(a, b, dims, preferred_element_type=F32)


def total_of(parts):
    total = parts[0].astype(F32)
    for part in parts[1:]:
        total = total + part.astype(F32)
    return total


def pick(step, table):
    value = jnp.int32(table[0])
    for i in range(1, len(table)):
        value = jnp.where(step == i, jnp.int32(table[i]), value)
    return value


EXPAND_SIDE = (0, 1, 0, 1, 0, 1, 0, 1)
EXPAND_FAR = (0, 0, 1, 1, 3, 3, 2, 2)
BACK_SIDE = (1, 1, 0, 1, 0, 0, 1, 0)
BACK_FAR = (2, 3, 2, 1, 3, 1, 0, 0)
BACK_STEP = {(side, far): i for i, (side, far) in enumerate(zip(BACK_SIDE, BACK_FAR))}
REL = (0, 1, 3, 2)
HALVES = (slice(0, 2), slice(2, 4))


def fused_kernel(
    lam, block_order, gain_hbm, queries_hbm, latent_hbm, rope_hbm, key_weight_hbm, value_weight_hbm, out_grad_hbm,
    query_grad, latent_out, rope_out,
    gain, queries, rope_in, rope_rows, key_weight, value_weight, out_grad,
    keys, key_pos, query_pos, q_cat, k_cat, values, scores, d_scores, tops, outs, totals, lowered, deltas, q_acc,
    part, from_s, from_a, from_b, from_plus, from_minus, middle, from_f, small, from_z, result,
    in_sem, z_send, z_recv, f_send, f_recv, l_send, l_recv, w_send, w_recv, s_send, s_recv,
    t_send, t_recv, a_send, a_recv, p_send, p_recv, m_send, m_recv, g_send, g_recv, y_send, y_recv, e_send, e_recv,
):
    me = Place()
    ctx = me.zh * 4 + me.x
    base, other = me.c * 4, me.o * 4
    mine = keys.at[base + me.last]
    row = pl.multiple_of(me.c * HALF + me.y * PIECE, PIECE)
    x_line = [me.at(x=lax.rem(me.x + d, 4)) for d in (1, 2, 3)]
    y_lines = [me.at(y=lax.rem(me.y + d, 4), c=c) for d in (1, 2, 3) for c in (0, 1)]
    z_line = [me.z_peer(d) for d in range(1, 8)]
    firsts = {d: me.first_peer(d) for d in (1, 2, 3)}
    lasts = {d: me.last_peer(d) for d in (1, 3)}
    sibling = me.sibling()
    barrier = pltpu.get_barrier_semaphore()
    for device in x_line + y_lines + z_line + [sibling]:
        pl.semaphore_signal(barrier, inc=1, device_id=device, device_id_type=MESH)

    first_piece = mine.at[me.zh, me.first]
    loads = [
        pltpu.make_async_copy(latent_hbm.at[pl.ds(row, PIECE)], first_piece.at[:, 0:D_LAT], in_sem.at[0]),
        pltpu.make_async_copy(rope_hbm, rope_in, in_sem.at[1]),
        pltpu.make_async_copy(queries_hbm, queries, in_sem.at[2]),
        pltpu.make_async_copy(key_weight_hbm, key_weight, in_sem.at[3]),
        pltpu.make_async_copy(value_weight_hbm, value_weight, in_sem.at[4]),
        pltpu.make_async_copy(out_grad_hbm, out_grad, in_sem.at[5]),
        pltpu.make_async_copy(gain_hbm, gain, in_sem.at[6]),
    ]
    for load in loads:
        load.start()

    chunk = lax.broadcasted_iota(jnp.int32, (CHUNKS, CHUNK), 0)
    lane = lax.broadcasted_iota(jnp.int32, (CHUNKS, CHUNK), 1)
    side, far = chunk // 4, chunk % 4
    k_z, k_first, k_r = lane // 64, (lane // 16) % 4, lane % 16
    slot = 2 * (k_z * 4 + jnp.where(side == 0, far, k_first)) + side
    held = jnp.zeros((CHUNKS, CHUNK), jnp.int32)
    for i in range(32):
        held = jnp.where(slot == i, block_order[i], held)
    key_pos[...] = held * HALF + jnp.where(side == 0, k_first, far) * PIECE + k_r
    token = lax.broadcasted_iota(jnp.int32, (ROWS, CHUNK), 0)
    query_pos[...] = (
        jnp.where(token < HALF, block_order[2 * ctx], block_order[2 * ctx + 1]) * HALF + token % HALF
    )
    tops[...] = jnp.full(tops.shape, -jnp.inf, F32)
    outs[...] = jnp.zeros(outs.shape, F32)
    totals[...] = jnp.zeros(totals.shape, F32)
    q_acc[...] = jnp.zeros(q_acc.shape, F32)

    loads[1].wait()
    rope_rows[:, 0:D_ROPE] = rope_in[...].astype(F32).T.astype(BF16)
    rope_rows[:, D_ROPE:128] = jnp.zeros((ROWS, 128 - D_ROPE), BF16)
    loads[0].wait()
    mine[me.zh, me.first, :, D_LAT:WIDE] = rope_rows[pl.ds(row, PIECE), :]
    pl.semaphore_wait(barrier, 17)

    def z_of(k):
        return lax.rem(me.zh + k, 4)

    forward_z = 2 * me.zl - 1
    ahead, across = lax.rem(me.zh + forward_z + 4, 4), z_of(2)
    z_to = [me.at(zh=ahead, zl=0), me.at(zh=ahead, zl=1), me.at(zh=across, zl=1 - me.zl)]

    def z_copy(i):
        return remote(first_piece, first_piece, z_send.at[i], z_recv.at[me.zh], z_to[i])

    def f_copy(k, d):
        piece = mine.at[z_of(k), me.first]
        i = k * 3 + d - 1
        return remote(piece, piece, f_send.at[i], f_recv.at[i], firsts[d])

    def l_copy(k, d):
        piece = mine.at[z_of(k)]
        i = (d // 2) * 4 + k
        return remote(piece, piece, l_send.at[i], l_recv.at[i], lasts[d])

    def w_copy(k, d):
        piece = keys.at[base + lax.rem(me.last + 4 - d, 4), z_of(k)]
        i = (d // 2) * 4 + k
        return remote(piece, piece, w_send.at[i], w_recv.at[i], lasts[d])

    W_PIECES = ((0, 3), (1, 3), (3, 1), (2, 1))

    def s_copy(d):
        piece = keys.at[base + lax.rem(me.last + d, 4)]
        return remote(piece, piece, s_send.at[d], s_recv.at[d], sibling)

    def f_sends(k):
        for d in (1, 3, 2):
            f_copy(k, d).start()

    def f_done(k):
        for d in (1, 2, 3):
            f_copy(k, d).wait_recv()
        for d in (1, 3):
            l_copy(k, d).start()

    def z_wait(k):
        piece = mine.at[z_of(k), me.first]
        remote(piece, piece, z_send.at[0], z_recv.at[z_of(k)], z_to[0]).wait_recv()

    for i in range(3):
        z_copy(i).start()
    f_sends(0)
    loads[2].wait()
    for h in range(MAPS):
        q_cat[h] = jnp.concatenate(
            [queries[:, h * D_QK : (h + 1) * D_QK], jnp.zeros((ROWS, 256 - D_QK), BF16)], axis=1
        )
    z_wait(1)
    f_sends(1)
    z_wait(3)
    f_sends(3)
    f_done(0)
    z_wait(2)
    f_sends(2)
    f_done(1)
    f_done(3)
    f_done(2)
    s_copy(0).start()
    for load in loads[3:]:
        load.wait()

    def expand(step, carry):
        @pl.when(step == 2)
        def _():
            for k in (0, 1, 3, 2):
                for d in (3, 1):
                    l_copy(k, d).wait_recv()
                    if (k, d) in W_PIECES:
                        w_copy(k, d).start()
            s_copy(1).start()
            s_copy(3).start()

        @pl.when(step == 6)
        def _():
            for k, d in W_PIECES:
                w_copy(k, d).wait_recv()
            s_copy(2).start()

        for i, d in ((1, 0), (3, 1), (5, 3), (7, 2)):

            @pl.when(step == i)
            def _(d=d):
                s_copy(d).wait_recv()

        theirs, distance = lax.rem(step, 2), pick(step, EXPAND_FAR)
        ours = 1 - theirs
        i = (base + lax.rem(me.last + distance, 4)) * ours + (other + lax.rem(me.first + distance, 4)) * theirs
        tokens = keys[i].reshape(CHUNK, WIDE)
        latent = tokens[:, 0:D_LAT]
        rope = tokens[:, D_LAT:WIDE]
        nope = dot(latent, key_weight[...]).astype(BF16)
        value = dot(latent, value_weight[...]).astype(BF16)
        seen = key_pos[pl.ds(i, 1), :] <= query_pos[...]
        for p in range(PAIRS_DEV):
            values[i, p] = value[:, p * PAIR_WIDTH : (p + 1) * PAIR_WIDTH]
        for h in range(MAPS):
            k_cat[i, h, :, 0:D_NOPE] = nope[:, h * D_NOPE : (h + 1) * D_NOPE]
            k_cat[i, h, :, D_NOPE:256] = rope
            tile = jnp.where(seen, dot(q_cat[h], k_cat[i, h], NT), -jnp.inf)
            scores[i, h] = tile
            tops[h] = jnp.maximum(tops[h], jnp.maximum(tile[:, 0:128], tile[:, 128:256]))
        return carry

    lax.fori_loop(0, CHUNKS, expand, 0)

    for h in range(MAPS):
        tops[h] = jnp.broadcast_to(jnp.max(tops[h], axis=1, keepdims=True), (ROWS, 128))

    def forward(i, carry):
        for p in range(PAIRS_DEV):
            both = []
            for m in range(2):
                h = 2 * p + m
                top = jnp.concatenate([tops[h], tops[h]], axis=1)
                weight = jnp.exp2((scores[i, h] - top) * (LOGIT_SCALE * LOG2E))
                scores[i, h] = weight
                totals[h] += weight[:, 0:128] + weight[:, 128:256]
                both.append(weight.astype(BF16))
            outs[p] += dot(jnp.concatenate(both, axis=0), values[i, p])
        return carry

    lax.fori_loop(0, CHUNKS, forward, 0)

    for p in range(PAIRS_DEV):
        lam_p = lam[p]
        maps = []
        for m in range(2):
            h = 2 * p + m
            inverse = 1.0 / jnp.sum(totals[h], axis=1, keepdims=True)
            totals[h] = jnp.broadcast_to(inverse, (ROWS, 128))
            maps.append(outs[p, m * ROWS : (m + 1) * ROWS] * inverse)
        mixed = maps[0] - lam_p * maps[1]
        inv_root = lax.rsqrt(jnp.mean(mixed * mixed, axis=1, keepdims=True) + EPS)
        normed = mixed * inv_root
        scaled = out_grad[:, p * PAIR_WIDTH : (p + 1) * PAIR_WIDTH].astype(F32) * gain[
            :, p * PAIR_WIDTH : (p + 1) * PAIR_WIDTH
        ]
        d_mixed = (scaled - normed * jnp.mean(scaled * normed, axis=1, keepdims=True)) * inv_root
        lowered[p] = d_mixed.astype(BF16)
        deltas[2 * p] = jnp.broadcast_to(jnp.sum(d_mixed * maps[0], axis=1, keepdims=True), (ROWS, 128))
        deltas[2 * p + 1] = jnp.broadcast_to(
            -lam_p * jnp.sum(d_mixed * maps[1], axis=1, keepdims=True), (ROWS, 128)
        )

    def t_copy(d):
        return remote(part.at[BACK_STEP[1, d]], from_s.at[d], t_send.at[d], t_recv.at[d], sibling)

    def a_copy(h):
        piece = part.at[BACK_STEP[0, 2], HALVES[h]]
        return remote(piece, (from_a, from_b)[h], a_send.at[h], a_recv.at[h], lasts[(1, 3)[h]])

    def p_copy(h):
        there = from_minus.at[HALVES[h]]
        return remote(part.at[BACK_STEP[0, 1], HALVES[h]], there, p_send.at[h], p_recv.at[h], lasts[1])

    def m_copy(h):
        there = from_plus.at[HALVES[h]]
        return remote(part.at[BACK_STEP[0, 3], HALVES[h]], there, m_send.at[h], m_recv.at[h], lasts[3])

    def add_up(d, h, extra=None):
        there = part.at[BACK_STEP[0, d], HALVES[h]]
        terms = [there[...], from_s[d, HALVES[h]]]
        if extra is not None:
            terms.append(extra[...])
        there[...] = total_of(terms).astype(BF16)

    def backward(step, carry):
        theirs, distance = pick(step, BACK_SIDE), pick(step, BACK_FAR)
        ours = 1 - theirs
        i = (base + lax.rem(me.last + distance, 4)) * ours + (other + lax.rem(me.first + distance, 4)) * theirs
        d_nope = []
        d_value = []
        d_rope = jnp.zeros((CHUNK, 128), F32)
        for p in range(PAIRS_DEV):
            lam_p = lam[p]
            grad = lowered[p]
            through = dot(grad, values[i, p], NT)
            probs = []
            for m in range(2):
                h = 2 * p + m
                probs.append(scores[i, h] * jnp.concatenate([totals[h], totals[h]], axis=1))
            d_value.append(dot((probs[0] - lam_p * probs[1]).astype(BF16), grad, TN).astype(BF16))
            for m in range(2):
                h = 2 * p + m
                delta = jnp.concatenate([deltas[h], deltas[h]], axis=1)
                inner = through if m == 0 else -lam_p * through
                d_score = (probs[m] * (inner - delta)).astype(BF16)
                d_scores[i, h] = d_score
                d_key = dot(d_score, q_cat[h], TN) * LOGIT_SCALE
                d_nope.append(d_key[:, 0:D_NOPE].astype(BF16))
                d_rope = d_rope + d_key[:, D_NOPE:256]
        d_latent = dot(jnp.concatenate(d_nope, axis=1), key_weight[...], NT)
        d_latent = d_latent + dot(jnp.concatenate(d_value, axis=1), value_weight[...], NT)
        part[step, :, :, :, 0:D_LAT] = d_latent.astype(BF16).reshape(4, 4, PIECE, D_LAT)
        part[step, :, :, :, D_LAT:WIDE] = d_rope.astype(BF16).reshape(4, 4, PIECE, WIDE - D_LAT)

        for d in (2, 3, 1, 0):

            @pl.when(step == BACK_STEP[1, d])
            def _(d=d):
                t_copy(d).start()

        @pl.when(step == BACK_STEP[0, 2])
        def _():
            t_copy(2).wait_recv()
            for h in range(2):
                add_up(2, h)
                a_copy(h).start()

        @pl.when(step == BACK_STEP[0, 3])
        def _():
            t_copy(3).wait_recv()
            add_up(3, 0)
            m_copy(0).start()

        @pl.when(step == BACK_STEP[0, 1])
        def _():
            t_copy(1).wait_recv()
            add_up(1, 1)
            p_copy(1).start()
            a_copy(1).wait_recv()
            add_up(3, 1, from_b)
            m_copy(1).start()
            a_copy(0).wait_recv()
            add_up(1, 0, from_a)
            p_copy(0).start()

        return carry

    lax.fori_loop(0, CHUNKS, backward, 0)

    def to_queries(i, carry):
        for h in range(MAPS):
            q_acc[h] += dot(d_scores[i, h], k_cat[i, h])
        return carry

    lax.fori_loop(0, CHUNKS, to_queries, 0)
    for h in range(MAPS):
        query_grad[:, h * D_QK : (h + 1) * D_QK] = (q_acc[h, :, 0:D_QK] * LOGIT_SCALE).astype(BF16)

    def g_copy(h, d):
        piece = middle.at[HALVES[h], lax.rem(me.first + d, 4)]
        i = h * 3 + d - 1
        return remote(piece, from_f.at[d - 1, HALVES[h]], g_send.at[i], g_recv.at[i], firsts[d])

    t_copy(0).wait_recv()
    for h in (1, 0):
        p_copy(h).wait_recv()
        m_copy(h).wait_recv()
        middle[HALVES[h]] = total_of(
            [part[BACK_STEP[0, 0], HALVES[h]], from_s[0, HALVES[h]], from_minus[HALVES[h]], from_plus[HALVES[h]]]
        ).astype(BF16)
        for d in (2, 1, 3):
            g_copy(h, d).start()
    for h in (1, 0):
        for d in (1, 3, 2):
            g_copy(h, d).wait_recv()
        small[HALVES[h]] = total_of(
            [middle[HALVES[h], me.first]] + [from_f[d, HALVES[h]] for d in range(3)]
        ).astype(BF16)
    z_mine = me.zh * 2 + me.zl

    def y_copy(d):
        source = small.at[lax.div(lax.rem(z_mine + d, 8), 2)]
        return remote(source, from_z.at[z_mine], y_send.at[d - 1], y_recv.at[z_mine], z_line[d - 1])

    for d in (4, 3, 5, 2, 6, 1, 7):
        y_copy(d).start()
    from_z[z_mine] = small[me.zh]
    for d in range(1, 8):
        z = lax.rem(z_mine + d, 8)
        there = from_z.at[z]
        remote(there, there, y_send.at[0], y_recv.at[z], z_line[0]).wait_recv()
    place = me.c * 4 + me.y
    result[place] = total_of([from_z[z] for z in range(8)]).astype(BF16)
    ends = y_lines + [sibling]

    def e_copy(i):
        return remote(result.at[place], result.at[place], e_send.at[i], e_recv.at[place], ends[i])

    for i in (2, 3, 0, 1, 4, 5, 6):
        e_copy(i).start()
    for d in range(1, 8):
        there = result.at[lax.rem(place + d, 8)]
        remote(there, there, e_send.at[0], e_recv.at[lax.rem(place + d, 8)], sibling).wait_recv()
    everything = result[...].reshape(ROWS, WIDE)
    latent_out[...] = everything[:, 0:D_LAT]
    rope_out[...] = everything[:, D_LAT:WIDE].astype(F32).T[0:D_ROPE].astype(BF16)

    sent = [z_copy(i) for i in range(3)] + [s_copy(d) for d in range(4)] + [t_copy(d) for d in range(4)]
    sent += [f_copy(k, d) for k in range(4) for d in (1, 2, 3)] + [l_copy(k, d) for k in range(4) for d in (1, 3)]
    sent += [w_copy(k, d) for k, d in W_PIECES]
    sent += [make(h) for make in (a_copy, p_copy, m_copy) for h in range(2)]
    sent += [g_copy(h, d) for h in range(2) for d in (1, 2, 3)]
    sent += [y_copy(d) for d in range(1, 8)] + [e_copy(i) for i in range(7)]
    for copy in sent:
        copy.wait_send()


VMEM = pl.BlockSpec(memory_space=pltpu.VMEM)
SMEM = pl.BlockSpec(memory_space=pltpu.SMEM)
ANY = pl.BlockSpec(memory_space=pl.ANY)
DMA = pltpu.SemaphoreType.DMA


def fused(lam, block_order, gain, queries, latent, rope_t, key_weight, value_weight, out_grad):
    piece = (PIECE, WIDE)
    return pl.pallas_call(
        fused_kernel,
        out_shape=(
            jax.ShapeDtypeStruct((ROWS, MAPS * D_QK), BF16),
            jax.ShapeDtypeStruct((ROWS, D_LAT), BF16),
            jax.ShapeDtypeStruct((D_ROPE, ROWS), BF16),
        ),
        in_specs=[SMEM, SMEM] + [ANY] * 7,
        out_specs=(VMEM, VMEM, VMEM),
        scratch_shapes=[
            pltpu.VMEM((1, 512), F32),
            pltpu.VMEM((ROWS, MAPS * D_QK), BF16),
            pltpu.VMEM((D_ROPE, ROWS), BF16),
            pltpu.VMEM((ROWS, 128), BF16),
            pltpu.VMEM((D_LAT, 512), BF16),
            pltpu.VMEM((D_LAT, 512), BF16),
            pltpu.VMEM((ROWS, 512), BF16),
            pltpu.VMEM((CHUNKS, 4, 4) + piece, BF16),
            pltpu.VMEM((CHUNKS, CHUNK), jnp.int32),
            pltpu.VMEM((ROWS, CHUNK), jnp.int32),
            pltpu.VMEM((MAPS, ROWS, 256), BF16),
            pltpu.VMEM((CHUNKS, MAPS, CHUNK, 256), BF16),
            pltpu.VMEM((CHUNKS, PAIRS_DEV, CHUNK, PAIR_WIDTH), BF16),
            pltpu.VMEM((CHUNKS, MAPS, ROWS, CHUNK), F32),
            pltpu.VMEM((CHUNKS, MAPS, ROWS, CHUNK), BF16),
            pltpu.VMEM((MAPS, ROWS, 128), F32),
            pltpu.VMEM((PAIRS_DEV, 2 * ROWS, PAIR_WIDTH), F32),
            pltpu.VMEM((MAPS, ROWS, 128), F32),
            pltpu.VMEM((PAIRS_DEV, ROWS, PAIR_WIDTH), BF16),
            pltpu.VMEM((MAPS, ROWS, 128), F32),
            pltpu.VMEM((MAPS, ROWS, 256), F32),
            pltpu.VMEM((CHUNKS, 4, 4) + piece, BF16),
            pltpu.VMEM((4, 4, 4) + piece, BF16),
            pltpu.VMEM((2, 4) + piece, BF16),
            pltpu.VMEM((2, 4) + piece, BF16),
            pltpu.VMEM((4, 4) + piece, BF16),
            pltpu.VMEM((4, 4) + piece, BF16),
            pltpu.VMEM((4, 4) + piece, BF16),
            pltpu.VMEM((3, 4) + piece, BF16),
            pltpu.VMEM((4,) + piece, BF16),
            pltpu.VMEM((8,) + piece, BF16),
            pltpu.VMEM((8,) + piece, BF16),
        ]
        + [
            DMA((n,))
            for n in (7, 3, 4, 12, 12, 8, 8, 8, 8, 4, 4, 4, 4, 2, 2, 2, 2, 2, 2, 6, 6, 7, 8, 7, 8)
        ],
        compiler_params=pltpu.CompilerParams(
            collective_id=0, has_side_effects=True, vmem_limit_bytes=56 << 20
        ),
        name="fused",
    )(lam, block_order, gain, queries, latent, rope_t, key_weight, value_weight, out_grad)


def on_device(
    queries, latent, rope_key, key_weight, value_weight, lambda_pair, norm_gain, out_grad, block_order
):
    query_grad, latent_grad, rope_grad = fused(
        lambda_pair, block_order, norm_gain.reshape(1, -1), queries, latent, rope_key.T,
        key_weight, value_weight, out_grad,
    )
    return (query_grad, latent_grad, rope_grad.T)


def solution(mesh):
    return jax.shard_map(
        on_device,
        mesh=mesh,
        in_specs=(
            P("ctx", "head"),
            P("ctx", None),
            P("ctx", None),
            P(None, "head"),
            P(None, "head"),
            P("head"),
            P("head"),
            P("ctx", "head"),
            P(),
        ),
        out_specs=(P("ctx", "head"), P("ctx", None), P("ctx", None)),
        check_vma=False,
    )
```

time: 93.7 us -> 65.4 us (0.70)
  Pallas kernels: 84.8 us -> 61.5 us
  other arithmetic: 2.72 us -> 0 us
  local copies, waits for them, and re-layouts: 5.21 us -> 2.98 us
    pallas_call x3 -> x1, Pallas kernels: 84.8 us -> 61.5 us  [fused(): pl.pallas_call(fused_kernel, out_shape=(jax.ShapeDtypeStruct((ROWS, MAPS...]
    reduce_sum x2 -> x0, other arithmetic: 1.68 us -> none  [the longest x1 0.93 us: on_device(): mine = jnp.sum(jnp.where(hot, block_order[None, :], 0), axis=1)]
    unnamed x19 -> x7, local copies, waits for them, and re-layouts: 4.59 us -> 2.98 us
where the time goes in v2:
time: 65.4 us; the launch traced here: 65.2 us
  Pallas kernels  61.5 us (94%)
  local copies, waits for them, and re-layouts  2.98 us (5%)
    pallas_call x1, Pallas kernels, fused(): pl.pallas_call(fused_kernel, out_shape=(jax.ShapeDtypeStruct((ROWS, MAPS...  61.5 us
    unnamed x7, local copies, waits for them, and re-layouts  2.98 us

profile of v2, /device:TPU:1, one launch (start us, length us, event | category | flops | bytes accessed | tf_op | source)
XLA Modules:
  0.0 65.2 jit_solution(3473832697807520131)
XLA Ops:
  0.6 61.5 %fused.1 = (bf16[128,768]{1,0:T(8,128)(2,1)}, bf16[128,512]{1,0:T(8,128)(2,1)}, bf16[64,128]{1,0:T(8,128)(2,1)}) custom-call(f32[2]{0:T(128)} %lam.1, s32[32]{0:T(128)} %block_order.1, f32[1,512]{1,0:T(1,128)} %bitcast.5, bf16[128,768]{1,0:T(8,128)(2,1)} %queries_hbm.1, bf16[128,512]{1,0:T(8,128)(2,1)} %latent_hbm.1, bf16[64,128]{1,0:T(8,128)(2,1)} %bitcast.4, ...), custom_call_target="tpu_custom_call" | custom-call | tf_op jit(solution)/shard_map/fused/pallas_call | solution.py:485
  62.2 0.0 copy-start
  62.2 1.7 %copy.15 = bf16[128,768]{1,0:T(8,128)(2,1)} copy(bf16[128,768]{1,0:T(8,128)(2,1)} %get-tuple-element.12) | data formatting | bytes 393216
  63.8 0.0 copy-done
  63.9 0.0 copy-start.1
  63.9 0.7 %copy.16 = bf16[128,512]{1,0:T(8,128)(2,1)} copy(bf16[128,512]{1,0:T(8,128)(2,1)S(1)} %copy-done) | data formatting | bytes 262144
  64.5 0.1 copy-done.1
  64.6 0.6 copy.17
Async XLA Ops:
  62.2 1.7 %copy-start = (bf16[128,512]{1,0:T(8,128)(2,1)S(1)}, bf16[128,512]{1,0:T(8,128)(2,1)}, u32[]{:S(2)}) copy-start(bf16[128,512]{1,0:T(8,128)(2,1)} %get-tuple-element.13) | copy-start | bytes 393220
  63.9 0.7 %copy-start.1 = (bf16[64,128]{1,0:T(8,128)(2,1)S(1)}, bf16[64,128]{1,0:T(8,128)(2,1)}, u32[]{:S(2)}) copy-start(bf16[64,128]{1,0:T(8,128)(2,1)} %get-tuple-element.8) | copy-start | bytes 49156

commit v3 on v2

v3 whole, which is shorter than its diff:
```python
import functools

import jax
import jax.numpy as jnp
from jax import lax
from jax.experimental import pallas as pl
from jax.experimental.pallas import tpu as pltpu
from jax.sharding import PartitionSpec as P

MESH = pl.DeviceIdType.MESH
D_LAT = 512
D_NOPE = 128
D_ROPE = 64
D_QK = D_NOPE + D_ROPE
PAIR_WIDTH = 256
ROWS = 128
WIDE = 640
HALF = 64
CHUNKS = 8
CHUNK = 256
PIECE = 16
MAPS = 4
PAIRS_DEV = 2
LOGIT_SCALE = D_QK**-0.5
EXPONENT = LOGIT_SCALE * 1.4426950408889634
EPS = 1e-6
F32 = jnp.float32
BF16 = jnp.bfloat16


class Place:
    def __init__(self):
        ctx, head = lax.axis_index("ctx"), lax.axis_index("head")
        self.x, self.zh = lax.rem(ctx, 4), lax.div(ctx, 4)
        self.y = lax.div(head, 4)
        self.zl = lax.rem(lax.div(head, 2), 2)
        self.c = lax.rem(head, 2)
        self.o = 1 - self.c
        self.first = self.y * self.o + self.x * self.c
        self.last = self.x * self.o + self.y * self.c

    def at(self, x=None, y=None, zh=None, zl=None, c=None):
        x = self.x if x is None else x
        y = self.y if y is None else y
        zh = self.zh if zh is None else zh
        zl = self.zl if zl is None else zl
        c = self.c if c is None else c
        return (zh * 4 + x, y * 4 + zl * 2 + c)

    def first_peer(self, d):
        return self.at(x=lax.rem(self.x + d * self.c, 4), y=lax.rem(self.y + d * self.o, 4))

    def last_peer(self, d):
        return self.at(x=lax.rem(self.x + d * self.o, 4), y=lax.rem(self.y + d * self.c, 4))

    def z_peer(self, d):
        z = lax.rem(self.zh * 2 + self.zl + d, 8)
        return self.at(zh=lax.div(z, 2), zl=lax.rem(z, 2))

    def sibling(self):
        return self.at(c=self.o)


def remote(src, dst, send, recv, device):
    return pltpu.make_async_remote_copy(
        src_ref=src, dst_ref=dst, send_sem=send, recv_sem=recv, device_id=device, device_id_type=MESH
    )


def greet(devices, count):
    barrier = pltpu.get_barrier_semaphore()
    for device in devices:
        pl.semaphore_signal(barrier, inc=1, device_id=device, device_id_type=MESH)
    pl.semaphore_wait(barrier, count)


NT = (((1,), (1,)), ((), ()))
TN = (((0,), (0,)), ((), ()))


def dot(a, b, dims=None):
    if dims is None:
        return jnp.dot(a, b, preferred_element_type=F32)
    return lax.dot_general(a, b, dims, preferred_element_type=F32)


def total_of(parts):
    total = parts[0].astype(F32)
    for part in parts[1:]:
        total = total + part.astype(F32)
    return total


def pick(step, table):
    value = jnp.int32(table[0])
    for i in range(1, len(table)):
        value = jnp.where(step == i, jnp.int32(table[i]), value)
    return value


BACK_SIDE = (1, 1, 0, 0, 1, 1, 0, 0)
BACK_TURN = (3, 2, 3, 2, 1, 0, 1, 0)
BACK_STEP = {(side, turn): i for i, (side, turn) in enumerate(zip(BACK_SIDE, BACK_TURN))}


def fused_kernel(
    lam_hbm, order_hbm, gain_hbm, queries_hbm, latent_hbm, rope_hbm, key_weight_hbm, value_weight_hbm, out_grad_hbm,
    query_hbm, latent_out_hbm, rope_out_hbm,
    query_grad, latent_out, rope_out, lam, block_order, gain, queries, rope_in, rope_rows, key_weight, value_weight, out_grad,
    keys, key_pos, query_pos, q_cat, k_cat, values, scores, d_scores, tops, tops_then, outs, totals, lowered, deltas, q_acc,
    part, from_s, from_l, middle, from_f, small, from_z, result,
    in_sem, out_sem, f_send, f_recv, z_send, z_recv, l_send, l_recv, s_send, s_recv,
    t_send, t_recv, p_send, p_recv, g_send, g_recv, y_send, y_recv, e_send, e_recv,
):
    me = Place()
    ctx = me.zh * 4 + me.x
    base, other = me.c * 4, me.o * 4
    x_line = [me.at(x=lax.rem(me.x + d, 4)) for d in (1, 2, 3)]
    y_lines = [me.at(y=lax.rem(me.y + d, 4), c=c) for d in (1, 2, 3) for c in (0, 1)]
    z_line = [me.z_peer(d) for d in range(1, 8)]
    firsts = {d: me.first_peer(d) for d in (1, 2, 3)}
    lasts = {d: me.last_peer(d) for d in (1, 2, 3)}
    sibling = me.sibling()
    barrier = pltpu.get_barrier_semaphore()
    for device in x_line + y_lines + z_line + [sibling]:
        pl.semaphore_signal(barrier, inc=1, device_id=device, device_id_type=MESH)

    near = lax.rem(me.zh + 3 - 2 * me.zl, 4)
    z_order = [me.zh, near, lax.rem(me.zh + 1 + 2 * me.zl, 4), lax.rem(me.zh + 2, 4)]
    my_rows = keys.at[base + me.zh, me.last]
    my_piece = my_rows.at[me.first]
    loads = [
        pltpu.make_async_copy(order_hbm, block_order, in_sem.at[0]),
        pltpu.make_async_copy(lam_hbm, lam, in_sem.at[1]),
        pltpu.make_async_copy(rope_hbm, rope_in, in_sem.at[2]),
        pltpu.make_async_copy(queries_hbm, queries, in_sem.at[3]),
        pltpu.make_async_copy(key_weight_hbm, key_weight, in_sem.at[4]),
        pltpu.make_async_copy(value_weight_hbm, value_weight, in_sem.at[5]),
        pltpu.make_async_copy(out_grad_hbm, out_grad, in_sem.at[6]),
        pltpu.make_async_copy(gain_hbm, gain, in_sem.at[7]),
    ]
    whole_load = pltpu.make_async_copy(
        latent_hbm.at[pl.ds(0, 4)], my_rows.at[:, :, pl.ds(0, D_LAT)], in_sem.at[8]
    )
    piece_load = pltpu.make_async_copy(
        latent_hbm.at[4 + me.y], my_piece.at[:, pl.ds(0, D_LAT)], in_sem.at[8]
    )

    @pl.when(me.c == 0)
    def _():
        whole_load.start()

    @pl.when(me.c == 1)
    def _():
        piece_load.start()

    loads[2].start()
    loads[0].start()
    loads[1].start()
    for load in loads[3:]:
        load.start()

    loads[2].wait()
    rope_rows[:, :, 0:D_ROPE] = rope_in[...].astype(F32).T.astype(BF16).reshape(8, PIECE, D_ROPE)
    rope_rows[:, :, D_ROPE:128] = jnp.zeros((8, PIECE, 128 - D_ROPE), BF16)

    @pl.when(me.c == 0)
    def _():
        whole_load.wait()
        my_rows[:, :, D_LAT:WIDE] = rope_rows[0:4]

    @pl.when(me.c == 1)
    def _():
        piece_load.wait()
        my_piece[:, D_LAT:WIDE] = rope_rows[4 + me.y]

    pl.semaphore_wait(barrier, 17)

    z_to = [
        me.at(zh=near, zl=1 - me.zl),
        me.at(zh=near, zl=me.zl),
        me.at(zh=z_order[3], zl=1 - me.zl),
    ]

    def f_copy(turn, d):
        piece = keys.at[base + z_order[turn], me.last, me.first]
        i = turn * 3 + d - 1
        return remote(piece, piece, f_send.at[i], f_recv.at[i], firsts[d])

    def rows_copy(i):
        return remote(my_rows, my_rows, z_send.at[i], z_recv.at[me.zh], z_to[i])

    def piece_copy(i):
        return remote(my_piece, my_piece, z_send.at[i], z_recv.at[me.zh], z_to[i])

    def rows_wait(turn):
        rows = keys.at[base + z_order[turn], me.last]
        remote(rows, rows, z_send.at[0], z_recv.at[z_order[turn]], z_to[0]).wait_recv()

    def piece_wait(turn):
        piece = keys.at[base + z_order[turn], me.last, me.first]
        remote(piece, piece, z_send.at[0], z_recv.at[z_order[turn]], z_to[0]).wait_recv()

    def l_copy(turn, d):
        rows = keys.at[base + z_order[turn], me.last]
        i = turn * 3 + d - 1
        return remote(rows, rows, l_send.at[i], l_recv.at[i], lasts[d])

    def s_copy(turn):
        rows = keys.at[base + z_order[turn]]
        return remote(rows, rows, s_send.at[turn], s_recv.at[turn], sibling)

    def l_sends(turn):
        for d in (2, 1, 3):
            l_copy(turn, d).start()

    def f_sends(turn):
        for d in (2, 1, 3):
            f_copy(turn, d).start()

    def f_done(turn):
        for d in (1, 3, 2):
            f_copy(turn, d).wait_recv()
        l_sends(turn)

    @pl.when(me.c == 0)
    def _():
        for i in range(3):
            rows_copy(i).start()
        l_sends(0)

    @pl.when(me.c == 1)
    def _():
        f_sends(0)
        for i in (2, 1, 0):
            piece_copy(i).start()

    loads[0].wait()
    chunk = lax.broadcasted_iota(jnp.int32, (CHUNKS, CHUNK), 0)
    lane = lax.broadcasted_iota(jnp.int32, (CHUNKS, CHUNK), 1)
    side, k_z = chunk // 4, chunk % 4
    k_last, k_first, k_r = lane // 64, (lane // 16) % 4, lane % 16
    slot = 2 * (k_z * 4 + jnp.where(side == 0, k_last, k_first)) + side
    held = jnp.zeros((CHUNKS, CHUNK), jnp.int32)
    for i in range(32):
        held = jnp.where(slot == i, block_order[i], held)
    key_pos[...] = held * HALF + jnp.where(side == 0, k_first, k_last) * PIECE + k_r
    token = lax.broadcasted_iota(jnp.int32, (ROWS, CHUNK), 0)
    query_pos[...] = (
        jnp.where(token < HALF, block_order[2 * ctx], block_order[2 * ctx + 1]) * HALF + token % HALF
    )
    tops[...] = jnp.full(tops.shape, -1e30, F32)
    outs[...] = jnp.zeros(outs.shape, F32)
    totals[...] = jnp.zeros(totals.shape, F32)
    q_acc[...] = jnp.zeros(q_acc.shape, F32)

    for load in loads[1:2] + loads[3:4]:
        load.wait()
    for h in range(MAPS):
        q_cat[h] = jnp.concatenate(
            [queries[:, h * D_QK : (h + 1) * D_QK], jnp.zeros((ROWS, 256 - D_QK), BF16)], axis=1
        )
    for load in loads[4:]:
        load.wait()

    @pl.when(me.c == 0)
    def _():
        for turn in (1, 2, 3):
            rows_wait(turn)
            l_sends(turn)

    @pl.when(me.c == 1)
    def _():
        f_done(0)
        for turn in (1, 2, 3):
            piece_wait(turn)
            f_sends(turn)
        for turn in (1, 2, 3):
            f_done(turn)

    def expand(step, carry):
        for turn in range(4):

            @pl.when(step == 2 * turn)
            def _(turn=turn):
                for d in (1, 3, 2):
                    l_copy(turn, d).wait_recv()
                s_copy(turn).start()

            @pl.when(step == 2 * turn + 1)
            def _(turn=turn):
                s_copy(turn).wait_recv()

        theirs = lax.rem(step, 2)
        i = base * (1 - theirs) + other * theirs + pick(lax.div(step, 2), z_order)
        tokens = keys[i].reshape(CHUNK, WIDE)
        latent = tokens[:, 0:D_LAT]
        rope = tokens[:, D_LAT:WIDE]
        nope = dot(latent, key_weight[...]).astype(BF16)
        value = dot(latent, value_weight[...]).astype(BF16)
        seen = key_pos[pl.ds(i, 1), :] <= query_pos[...]
        for p in range(PAIRS_DEV):
            values[i, p] = value[:, p * PAIR_WIDTH : (p + 1) * PAIR_WIDTH]
        for p in range(PAIRS_DEV):
            both, shrinks = [], []
            for m in range(2):
                h = 2 * p + m
                k_cat[i, h, :, 0:D_NOPE] = nope[:, h * D_NOPE : (h + 1) * D_NOPE]
                k_cat[i, h, :, D_NOPE:256] = rope
                tile = jnp.where(seen, dot(q_cat[h], k_cat[i, h], NT), -jnp.inf)
                top = jnp.maximum(tops[h], jnp.max(tile, axis=1, keepdims=True))
                shrink = jnp.exp2((tops[h] - top) * EXPONENT)
                weight = jnp.exp2((tile - jnp.concatenate([top, top], axis=1)) * EXPONENT)
                tops[h] = top
                tops_then[i, h] = top
                scores[i, h] = weight
                totals[h] = totals[h] * shrink + (weight[:, 0:128] + weight[:, 128:256])
                both.append(weight.astype(BF16))
                shrinks.append(jnp.concatenate([shrink, shrink], axis=1))
            outs[p] = outs[p] * jnp.concatenate(shrinks, axis=0) + dot(
                jnp.concatenate(both, axis=0), values[i, p]
            )
        return carry

    lax.fori_loop(0, CHUNKS, expand, 0)

    for p in range(PAIRS_DEV):
        lam_p = lam[p]
        maps = []
        for m in range(2):
            h = 2 * p + m
            inverse = 1.0 / jnp.sum(totals[h], axis=1, keepdims=True)
            totals[h] = jnp.broadcast_to(inverse, (ROWS, 128))
            maps.append(outs[p, m * ROWS : (m + 1) * ROWS] * inverse)
        mixed = maps[0] - lam_p * maps[1]
        inv_root = lax.rsqrt(jnp.mean(mixed * mixed, axis=1, keepdims=True) + EPS)
        normed = mixed * inv_root
        scaled = out_grad[:, p * PAIR_WIDTH : (p + 1) * PAIR_WIDTH].astype(F32) * gain[
            :, p * PAIR_WIDTH : (p + 1) * PAIR_WIDTH
        ]
        d_mixed = (scaled - normed * jnp.mean(scaled * normed, axis=1, keepdims=True)) * inv_root
        lowered[p] = d_mixed.astype(BF16)
        deltas[2 * p] = jnp.broadcast_to(jnp.sum(d_mixed * maps[0], axis=1, keepdims=True), (ROWS, 128))
        deltas[2 * p + 1] = jnp.broadcast_to(
            -lam_p * jnp.sum(d_mixed * maps[1], axis=1, keepdims=True), (ROWS, 128)
        )

    def t_copy(turn):
        return remote(part.at[BACK_STEP[1, turn]], from_s.at[turn], t_send.at[turn], t_recv.at[turn], sibling)

    def p_copy(turn, d):
        rows = part.at[BACK_STEP[0, turn], lax.rem(me.last + d, 4)]
        i = turn * 3 + d - 1
        return remote(rows, from_l.at[turn, d - 1], p_send.at[i], p_recv.at[i], lasts[d])

    def g_copy(turn, d):
        piece = middle.at[turn, lax.rem(me.first + d, 4)]
        i = turn * 3 + d - 1
        return remote(piece, from_f.at[turn, d - 1], g_send.at[i], g_recv.at[i], firsts[d])

    def add_own(turn):
        t_copy(turn).wait_recv()
        there = part.at[BACK_STEP[0, turn]]
        there[...] = total_of([there[...], from_s[turn]]).astype(BF16)
        for d in (2, 1, 3):
            p_copy(turn, d).start()

    def add_last(turn):
        for d in (1, 3, 2):
            p_copy(turn, d).wait_recv()
        middle[turn] = total_of(
            [part[BACK_STEP[0, turn], me.last]] + [from_l[turn, d] for d in range(3)]
        ).astype(BF16)
        for d in (2, 1, 3):
            g_copy(turn, d).start()

    def backward(step, carry):
        theirs = pick(step, BACK_SIDE)
        i = base * (1 - theirs) + other * theirs + pick(pick(step, BACK_TURN), z_order)
        d_nope = []
        d_value = []
        d_rope = jnp.zeros((CHUNK, 128), F32)
        for p in range(PAIRS_DEV):
            lam_p = lam[p]
            grad = lowered[p]
            through = dot(grad, values[i, p], NT)
            probs = []
            for m in range(2):
                h = 2 * p + m
                share = jnp.exp2((tops_then[i, h] - tops[h]) * EXPONENT) * totals[h]
                probs.append(scores[i, h] * jnp.concatenate([share, share], axis=1))
            d_value.append(dot((probs[0] - lam_p * probs[1]).astype(BF16), grad, TN).astype(BF16))
            for m in range(2):
                h = 2 * p + m
                delta = jnp.concatenate([deltas[h], deltas[h]], axis=1)
                inner = through if m == 0 else -lam_p * through
                d_score = (probs[m] * (inner - delta)).astype(BF16)
                d_scores[i, h] = d_score
                d_key = dot(d_score, q_cat[h], TN) * LOGIT_SCALE
                d_nope.append(d_key[:, 0:D_NOPE].astype(BF16))
                d_rope = d_rope + d_key[:, D_NOPE:256]
        d_latent = dot(jnp.concatenate(d_nope, axis=1), key_weight[...], NT)
        d_latent = d_latent + dot(jnp.concatenate(d_value, axis=1), value_weight[...], NT)
        part[step, :, :, :, 0:D_LAT] = d_latent.astype(BF16).reshape(4, 4, PIECE, D_LAT)
        part[step, :, :, :, D_LAT:WIDE] = d_rope.astype(BF16).reshape(4, 4, PIECE, WIDE - D_LAT)

        for turn in range(4):

            @pl.when(step == BACK_STEP[1, turn])
            def _(turn=turn):
                t_copy(turn).start()

            @pl.when(step == BACK_STEP[0, turn])
            def _(turn=turn):
                add_own(turn)

        return carry

    lax.fori_loop(0, CHUNKS, backward, 0)
    add_last(3)
    add_last(2)

    def to_queries(i, carry):
        for h in range(MAPS):
            q_acc[h] += dot(d_scores[i, h], k_cat[i, h])
        return carry

    lax.fori_loop(0, CHUNKS, to_queries, 0)
    for h in range(MAPS):
        query_grad[:, h * D_QK : (h + 1) * D_QK] = (q_acc[h, :, 0:D_QK] * LOGIT_SCALE).astype(BF16)

    stores = [
        pltpu.make_async_copy(query_grad, query_hbm, out_sem.at[0]),
        pltpu.make_async_copy(latent_out, latent_out_hbm, out_sem.at[1]),
        pltpu.make_async_copy(rope_out, rope_out_hbm, out_sem.at[2]),
    ]
    stores[0].start()
    z_mine = me.zh * 2 + me.zl

    def y_copy(turn, zl):
        i = turn * 2 + zl
        device = me.at(zh=z_order[turn], zl=zl)
        return remote(small.at[turn], from_z.at[z_mine], y_send.at[i], y_recv.at[z_mine], device)

    own_y = remote(
        small.at[0], from_z.at[z_mine], y_send.at[0], y_recv.at[z_mine], me.at(zl=1 - me.zl)
    )

    def add_first(turn):
        for d in (1, 3, 2):
            g_copy(turn, d).wait_recv()
        small[turn] = total_of(
            [middle[turn, me.first]] + [from_f[turn, d] for d in range(3)]
        ).astype(BF16)
        if turn:
            for zl in (0, 1):
                y_copy(turn, zl).start()
        else:
            own_y.start()

    add_first(3)
    add_first(2)
    add_last(1)
    add_last(0)
    add_first(1)
    add_first(0)
    from_z[z_mine] = small[0]
    for d in range(1, 8):
        z = lax.rem(z_mine + d, 8)
        there = from_z.at[z]
        remote(there, there, y_send.at[0], y_recv.at[z], z_line[0]).wait_recv()
    place = me.c * 4 + me.y
    result[place] = total_of([from_z[z] for z in range(8)]).astype(BF16)
    ends = y_lines + [sibling]

    def e_copy(i):
        return remote(result.at[place], result.at[place], e_send.at[i], e_recv.at[place], ends[i])

    for i in (2, 3, 0, 1, 4, 5, 6):
        e_copy(i).start()
    for d in range(1, 8):
        there = result.at[lax.rem(place + d, 8)]
        remote(there, there, e_send.at[0], e_recv.at[lax.rem(place + d, 8)], sibling).wait_recv()
    everything = result[...].reshape(ROWS, WIDE)
    latent_out[...] = everything[:, 0:D_LAT]
    rope_out[...] = everything[:, D_LAT:WIDE].astype(F32).T[0:D_ROPE].astype(BF16)
    stores[1].start()
    stores[2].start()

    @pl.when(me.c == 0)
    def _():
        for i in range(3):
            rows_copy(i).wait_send()

    @pl.when(me.c == 1)
    def _():
        for i in range(3):
            piece_copy(i).wait_send()
        for turn in range(4):
            for d in (1, 2, 3):
                f_copy(turn, d).wait_send()

    sent = [s_copy(turn) for turn in range(4)] + [t_copy(turn) for turn in range(4)]
    sent += [make(turn, d) for make in (l_copy, p_copy, g_copy) for turn in range(4) for d in (1, 2, 3)]
    sent += [y_copy(turn, zl) for turn in (1, 2, 3) for zl in (0, 1)] + [own_y]
    sent += [e_copy(i) for i in range(7)]
    for copy in sent:
        copy.wait_send()
    for store in stores:
        store.wait()


def copy_out(query_in, latent_in, rope_in, query_out, latent_out, rope_out, query, latent, rope, in_sem, out_sem):
    steps = [(query_in, query, query_out), (latent_in, latent, latent_out), (rope_in, rope, rope_out)]
    reads = [pltpu.make_async_copy(a, b, in_sem.at[i]) for i, (a, b, c) in enumerate(steps)]
    writes = [pltpu.make_async_copy(b, c, out_sem.at[i]) for i, (a, b, c) in enumerate(steps)]
    for read in reads:
        read.start()
    for read, write in zip(reads, writes):
        read.wait()
        write.start()
    for write in writes:
        write.wait()


VMEM = pl.BlockSpec(memory_space=pltpu.VMEM)
SMEM = pl.BlockSpec(memory_space=pltpu.SMEM)
ANY = pl.BlockSpec(memory_space=pl.ANY)
DMA = pltpu.SemaphoreType.DMA


OUTS = (
    jax.ShapeDtypeStruct((ROWS, MAPS * D_QK), BF16),
    jax.ShapeDtypeStruct((ROWS, D_LAT), BF16),
    jax.ShapeDtypeStruct((D_ROPE, ROWS), BF16),
)


def fused(*operands):
    piece = (PIECE, WIDE)
    outs = pl.pallas_call(
        fused_kernel,
        out_shape=OUTS,
        in_specs=[ANY] * 9,
        out_specs=(ANY, ANY, ANY),
        scratch_shapes=[pltpu.VMEM(out.shape, BF16) for out in OUTS]
        + [
            pltpu.SMEM((PAIRS_DEV,), F32),
            pltpu.SMEM((32,), jnp.int32),
            pltpu.VMEM((1, 512), F32),
            pltpu.VMEM((ROWS, MAPS * D_QK), BF16),
            pltpu.VMEM((D_ROPE, ROWS), BF16),
            pltpu.VMEM((8, PIECE, 128), BF16),
            pltpu.VMEM((D_LAT, 512), BF16),
            pltpu.VMEM((D_LAT, 512), BF16),
            pltpu.VMEM((ROWS, 512), BF16),
            pltpu.VMEM((CHUNKS, 4, 4) + piece, BF16),
            pltpu.VMEM((CHUNKS, CHUNK), jnp.int32),
            pltpu.VMEM((ROWS, CHUNK), jnp.int32),
            pltpu.VMEM((MAPS, ROWS, 256), BF16),
            pltpu.VMEM((CHUNKS, MAPS, CHUNK, 256), BF16),
            pltpu.VMEM((CHUNKS, PAIRS_DEV, CHUNK, PAIR_WIDTH), BF16),
            pltpu.VMEM((CHUNKS, MAPS, ROWS, CHUNK), F32),
            pltpu.VMEM((CHUNKS, MAPS, ROWS, CHUNK), BF16),
            pltpu.VMEM((MAPS, ROWS, 128), F32),
            pltpu.VMEM((CHUNKS, MAPS, ROWS, 128), F32),
            pltpu.VMEM((PAIRS_DEV, 2 * ROWS, PAIR_WIDTH), F32),
            pltpu.VMEM((MAPS, ROWS, 128), F32),
            pltpu.VMEM((PAIRS_DEV, ROWS, PAIR_WIDTH), BF16),
            pltpu.VMEM((MAPS, ROWS, 128), F32),
            pltpu.VMEM((MAPS, ROWS, 256), F32),
            pltpu.VMEM((CHUNKS, 4, 4) + piece, BF16),
            pltpu.VMEM((4, 4, 4) + piece, BF16),
            pltpu.VMEM((4, 3, 4) + piece, BF16),
            pltpu.VMEM((4, 4) + piece, BF16),
            pltpu.VMEM((4, 3) + piece, BF16),
            pltpu.VMEM((4,) + piece, BF16),
            pltpu.VMEM((8,) + piece, BF16),
            pltpu.VMEM((8,) + piece, BF16),
        ]
        + [DMA((n,)) for n in (9, 3, 12, 12, 3, 4, 12, 12, 4, 4, 4, 4, 12, 12, 12, 12, 8, 8, 7, 8)],
        compiler_params=pltpu.CompilerParams(
            collective_id=0, has_side_effects=True, vmem_limit_bytes=56 << 20
        ),
        name="fused",
    )(*operands)
    return pl.pallas_call(
        copy_out,
        out_shape=OUTS,
        in_specs=[ANY] * 3,
        out_specs=(ANY, ANY, ANY),
        scratch_shapes=[pltpu.VMEM(out.shape, BF16) for out in OUTS] + [DMA((3,)), DMA((3,))],
        name="copy_out",
    )(*outs)


def on_device(
    queries, latent, rope_key, key_weight, value_weight, lambda_pair, norm_gain, out_grad, block_order
):
    query_grad, latent_grad, rope_grad = fused(
        lambda_pair, block_order, norm_gain.reshape(1, -1), queries, latent.reshape(8, PIECE, D_LAT), rope_key.T,
        key_weight, value_weight, out_grad,
    )
    return (query_grad, latent_grad, rope_grad.T)


def solution(mesh):
    return jax.shard_map(
        on_device,
        mesh=mesh,
        in_specs=(
            P("ctx", "head"),
            P("ctx", None),
            P("ctx", None),
            P(None, "head"),
            P(None, "head"),
            P("head"),
            P("head"),
            P("ctx", "head"),
            P(),
        ),
        out_specs=(P("ctx", "head"), P("ctx", None), P("ctx", None)),
        check_vma=False,
    )
```

time: 65.4 us -> 58 us (0.89)
  Pallas kernels: 61.5 us -> 57.3 us
  local copies, waits for them, and re-layouts: 2.98 us -> 0 us
    pallas_call x1 -> x2, Pallas kernels: 61.5 us -> 57.3 us  [the longest x1 55.6 us: fused(): pl.pallas_call(fused_kernel, out_shape=OUTS, in_specs=[ANY] * 9, out_spec...]
    unnamed x7 -> x0, local copies, waits for them, and re-layouts: 2.98 us -> none
where the time goes in v3:
time: 58 us; the launch traced here: 57.9 us
  Pallas kernels  57.3 us (99%)
  between operations  0.64 us (1%)
    pallas_call x1, Pallas kernels, fused(): pl.pallas_call(fused_kernel, out_shape=OUTS, in_specs=[ANY] * 9, out_spec...  55.6 us
    pallas_call x1, Pallas kernels, fused(): pl.pallas_call(copy_out, out_shape=OUTS, in_specs=[ANY] * 3, out_specs=(A...  1.71 us

profile of v3, /device:TPU:1, one launch (start us, length us, event | category | flops | bytes accessed | tf_op | source)
XLA Modules:
  0.0 57.9 jit_solution(10817800925914517158)
XLA Ops:
  0.6 55.6 %fused.1 = (bf16[128,768]{1,0:T(8,128)(2,1)}, bf16[128,512]{1,0:T(8,128)(2,1)}, bf16[64,128]{1,0:T(8,128)(2,1)}) custom-call(f32[2]{0:T(128)} %lam_hbm.1, s32[32]{0:T(128)} %order_hbm.1, f32[1,512]{1,0:T(1,128)} %bitcast.6, bf16[128,768]{1,0:T(8,128)(2,1)} %queries_hbm.1, bf16[8,16,512]{2,1,0:T(8,128)(2,1)} %bitcast.4, bf16[64,128]{1,0:T(8,128)(2,1)} %bitcast.5, ...), custom_call_target="tpu_custom_call" | custom-call | tf_op jit(solution)/shard_map/fused/pallas_call | solution.py:541
  56.2 1.7 %copy_out.1 = (bf16[128,768]{1,0:T(8,128)(2,1)}, bf16[128,512]{1,0:T(8,128)(2,1)}, bf16[64,128]{1,0:T(8,128)(2,1)}) custom-call(bf16[128,768]{1,0:T(8,128)(2,1)} %get-tuple-element.9.query_in, bf16[128,512]{1,0:T(8,128)(2,1)} %get-tuple-element.10.latent_in, bf16[64,128]{1,0:T(8,128)(2,1)} %get-tuple-element.11.rope_in), custom_call_target="tpu_custom_call" | custom-call | tf_op jit(solution)/shard_map/copy_out/pallas_call | solution.py:587

commit v4 on v3

--- a/solution.py
+++ b/solution.py
@@ -98,31 +98,31 @@
     return value
 
 
-BACK_SIDE = (1, 1, 0, 0, 1, 1, 0, 0)
-BACK_TURN = (3, 2, 3, 2, 1, 0, 1, 0)
+BACK_SIDE = (1, 1, 0, 1, 0, 1, 0, 0)
+BACK_TURN = (3, 2, 3, 1, 2, 0, 1, 0)
 BACK_STEP = {(side, turn): i for i, (side, turn) in enumerate(zip(BACK_SIDE, BACK_TURN))}
 
 
 def fused_kernel(
     lam_hbm, order_hbm, gain_hbm, queries_hbm, latent_hbm, rope_hbm, key_weight_hbm, value_weight_hbm, out_grad_hbm,
-    query_hbm, latent_out_hbm, rope_out_hbm,
-    query_grad, latent_out, rope_out, lam, block_order, gain, queries, rope_in, rope_rows, key_weight, value_weight, out_grad,
-    keys, key_pos, query_pos, q_cat, k_cat, values, scores, d_scores, tops, tops_then, outs, totals, lowered, deltas, q_acc,
+    query_hbm, result_hbm,
+    query_grad, lam, block_order, gain, queries, rope_in, rope_rows, key_weight, value_weight, out_grad,
+    keys, key_pos, query_pos, q_cat, q_nope, q_rope, k_cat, values, scores, d_scores, tops, tops_then, outs, totals, lowered, deltas, q_acc,
     part, from_s, from_l, middle, from_f, small, from_z, result,
     in_sem, out_sem, f_send, f_recv, z_send, z_recv, l_send, l_recv, s_send, s_recv,
-    t_send, t_recv, p_send, p_recv, g_send, g_recv, y_send, y_recv, e_send, e_recv,
+    t_send, t_recv, p_send, p_recv, g_send, g_recv, y_send, y_recv, e_send, e_recv, r_send, r_recv,
 ):
     me = Place()
     ctx = me.zh * 4 + me.x
     base, other = me.c * 4, me.o * 4
     x_line = [me.at(x=lax.rem(me.x + d, 4)) for d in (1, 2, 3)]
-    y_lines = [me.at(y=lax.rem(me.y + d, 4), c=c) for d in (1, 2, 3) for c in (0, 1)]
+    y_line = [me.at(y=lax.rem(me.y + d, 4)) for d in (1, 2, 3)]
     z_line = [me.z_peer(d) for d in range(1, 8)]
     firsts = {d: me.first_peer(d) for d in (1, 2, 3)}
     lasts = {d: me.last_peer(d) for d in (1, 2, 3)}
     sibling = me.sibling()
     barrier = pltpu.get_barrier_semaphore()
-    for device in x_line + y_lines + z_line + [sibling]:
+    for device in x_line + y_line + z_line + [sibling]:
         pl.semaphore_signal(barrier, inc=1, device_id=device, device_id_type=MESH)
 
     near = lax.rem(me.zh + 3 - 2 * me.zl, 4)
@@ -174,7 +174,7 @@
         piece_load.wait()
         my_piece[:, D_LAT:WIDE] = rope_rows[4 + me.y]
 
-    pl.semaphore_wait(barrier, 17)
+    pl.semaphore_wait(barrier, 14)
 
     z_to = [
         me.at(zh=near, zl=1 - me.zl),
@@ -201,13 +201,16 @@
         piece = keys.at[base + z_order[turn], me.last, me.first]
         remote(piece, piece, z_send.at[0], z_recv.at[z_order[turn]], z_to[0]).wait_recv()
 
+    def z_at(turn):
+        return z_order[turn] if isinstance(turn, int) else pick(turn, z_order)
+
     def l_copy(turn, d):
-        rows = keys.at[base + z_order[turn], me.last]
+        rows = keys.at[base + z_at(turn), me.last]
         i = turn * 3 + d - 1
         return remote(rows, rows, l_send.at[i], l_recv.at[i], lasts[d])
 
     def s_copy(turn):
-        rows = keys.at[base + z_order[turn]]
+        rows = keys.at[base + z_at(turn)]
         return remote(rows, rows, s_send.at[turn], s_recv.at[turn], sibling)
 
     def l_sends(turn):
@@ -260,12 +263,16 @@
         q_cat[h] = jnp.concatenate(
             [queries[:, h * D_QK : (h + 1) * D_QK], jnp.zeros((ROWS, 256 - D_QK), BF16)], axis=1
         )
+        rows, columns = pl.ds(h % 2 * ROWS, ROWS), h % 2 * D_NOPE
+        q_nope[h // 2, rows, columns : columns + D_NOPE] = q_cat[h, :, 0:D_NOPE]
+        q_nope[h // 2, rows, D_NOPE - columns : 2 * D_NOPE - columns] = jnp.zeros((ROWS, D_NOPE), BF16)
+        q_rope[h * ROWS : (h + 1) * ROWS, :] = q_cat[h, :, D_NOPE:256]
     for load in loads[4:]:
         load.wait()
 
     @pl.when(me.c == 0)
     def _():
-        for turn in (1, 2, 3):
+        for turn in (1, 2):
             rows_wait(turn)
             l_sends(turn)
 
@@ -275,54 +282,76 @@
         for turn in (1, 2, 3):
             piece_wait(turn)
             f_sends(turn)
-        for turn in (1, 2, 3):
+        for turn in (1, 2):
             f_done(turn)
 
-    def expand(step, carry):
-        for turn in range(4):
-
-            @pl.when(step == 2 * turn)
-            def _(turn=turn):
-                for d in (1, 3, 2):
-                    l_copy(turn, d).wait_recv()
-                s_copy(turn).start()
-
-            @pl.when(step == 2 * turn + 1)
-            def _(turn=turn):
-                s_copy(turn).wait_recv()
-
-        theirs = lax.rem(step, 2)
-        i = base * (1 - theirs) + other * theirs + pick(lax.div(step, 2), z_order)
-        tokens = keys[i].reshape(CHUNK, WIDE)
-        latent = tokens[:, 0:D_LAT]
-        rope = tokens[:, D_LAT:WIDE]
+    def absorb(chunks):
+        spans = [slice(n * CHUNK, (n + 1) * CHUNK) for n in range(len(chunks))]
+        tokens = [keys[i].reshape(CHUNK, WIDE) for i in chunks]
+        latent = jnp.concatenate([part[:, 0:D_LAT] for part in tokens], axis=0)
         nope = dot(latent, key_weight[...]).astype(BF16)
         value = dot(latent, value_weight[...]).astype(BF16)
-        seen = key_pos[pl.ds(i, 1), :] <= query_pos[...]
-        for p in range(PAIRS_DEV):
-            values[i, p] = value[:, p * PAIR_WIDTH : (p + 1) * PAIR_WIDTH]
+        seen = [key_pos[pl.ds(i, 1), :] <= query_pos[...] for i in chunks]
+        for i, span, part in zip(chunks, spans, tokens):
+            for p in range(PAIRS_DEV):
+                values[i, p] = value[span, p * PAIR_WIDTH : (p + 1) * PAIR_WIDTH]
+            for h in range(MAPS):
+                k_cat[i, h, :, 0:D_NOPE] = nope[span, h * D_NOPE : (h + 1) * D_NOPE]
+                k_cat[i, h, :, D_NOPE:256] = part[:, D_LAT:WIDE]
         for p in range(PAIRS_DEV):
             both, shrinks = [], []
             for m in range(2):
                 h = 2 * p + m
-                k_cat[i, h, :, 0:D_NOPE] = nope[:, h * D_NOPE : (h + 1) * D_NOPE]
-                k_cat[i, h, :, D_NOPE:256] = rope
-                tile = jnp.where(seen, dot(q_cat[h], k_cat[i, h], NT), -jnp.inf)
-                top = jnp.maximum(tops[h], jnp.max(tile, axis=1, keepdims=True))
+                tiles = [
+                    jnp.where(mask, dot(q_cat[h], k_cat[i, h], NT), -jnp.inf) for i, mask in zip(chunks, seen)
+                ]
+                highest = functools.reduce(jnp.maximum, tiles)
+                top = jnp.maximum(tops[h], jnp.max(highest, axis=1, keepdims=True))
                 shrink = jnp.exp2((tops[h] - top) * EXPONENT)
-                weight = jnp.exp2((tile - jnp.concatenate([top, top], axis=1)) * EXPONENT)
+                wide_top = jnp.concatenate([top, top], axis=1)
+                weights = [jnp.exp2((tile - wide_top) * EXPONENT) for tile in tiles]
                 tops[h] = top
-                tops_then[i, h] = top
-                scores[i, h] = weight
-                totals[h] = totals[h] * shrink + (weight[:, 0:128] + weight[:, 128:256])
-                both.append(weight.astype(BF16))
+                total = functools.reduce(jnp.add, weights)
+                totals[h] = totals[h] * shrink + (total[:, 0:128] + total[:, 128:256])
+                for i, weight in zip(chunks, weights):
+                    tops_then[i, h] = top
+                    scores[i, h] = weight
+                both.append(jnp.concatenate([weight.astype(BF16) for weight in weights], axis=1))
                 shrinks.append(jnp.concatenate([shrink, shrink], axis=1))
             outs[p] = outs[p] * jnp.concatenate(shrinks, axis=0) + dot(
-                jnp.concatenate(both, axis=0), values[i, p]
+                jnp.concatenate(both, axis=0), value[:, p * PAIR_WIDTH : (p + 1) * PAIR_WIDTH]
             )
+
+    def own_ready(turn):
+        for d in (1, 3, 2):
+            l_copy(turn, d).wait_recv()
+        s_copy(turn).start()
+
+    own_ready(0)
+    absorb([base + z_order[0]])
+
+    @pl.when(me.c == 0)
+    def _():
+        rows_wait(3)
+
+    @pl.when(me.c == 1)
+    def _():
+        for d in (1, 3, 2):
+            f_copy(3, d).wait_recv()
+
+    for d in (2, 1, 3):
+        l_copy(1, d).wait_send()
+    l_sends(3)
+
+    def expand(turn, carry):
+        own_ready(turn)
+        s_copy(turn - 1).wait_recv()
+        absorb([other + z_at(turn - 1), base + z_at(turn)])
         return carry
 
-    lax.fori_loop(0, CHUNKS, expand, 0)
+    lax.fori_loop(1, 4, expand, 0)
+    s_copy(3).wait_recv()
+    absorb([other + z_order[3]])
 
     for p in range(PAIRS_DEV):
         lam_p = lam[p]
@@ -374,12 +403,12 @@
         for d in (2, 1, 3):
             g_copy(turn, d).start()
 
-    def backward(step, carry):
+    def chunk_grads(step):
         theirs = pick(step, BACK_SIDE)
         i = base * (1 - theirs) + other * theirs + pick(pick(step, BACK_TURN), z_order)
         d_nope = []
         d_value = []
-        d_rope = jnp.zeros((CHUNK, 128), F32)
+        d_all = []
         for p in range(PAIRS_DEV):
             lam_p = lam[p]
             grad = lowered[p]
@@ -387,36 +416,44 @@
             probs = []
             for m in range(2):
                 h = 2 * p + m
-                share = jnp.exp2((tops_then[i, h] - tops[h]) * EXPONENT) * totals[h]
+                share = jnp.exp2((tops_then[i, h] - tops[h]) * EXPONENT) * (totals[h] * LOGIT_SCALE)
                 probs.append(scores[i, h] * jnp.concatenate([share, share], axis=1))
-            d_value.append(dot((probs[0] - lam_p * probs[1]).astype(BF16), grad, TN).astype(BF16))
+            merged = probs[0] * (1 / LOGIT_SCALE) - probs[1] * (lam_p * (1 / LOGIT_SCALE))
+            d_value.append(dot(merged.astype(BF16), grad, TN).astype(BF16))
+            pair = []
             for m in range(2):
                 h = 2 * p + m
                 delta = jnp.concatenate([deltas[h], deltas[h]], axis=1)
                 inner = through if m == 0 else -lam_p * through
                 d_score = (probs[m] * (inner - delta)).astype(BF16)
                 d_scores[i, h] = d_score
-                d_key = dot(d_score, q_cat[h], TN) * LOGIT_SCALE
-                d_nope.append(d_key[:, 0:D_NOPE].astype(BF16))
-                d_rope = d_rope + d_key[:, D_NOPE:256]
+                pair.append(d_score)
+            d_nope.append(dot(jnp.concatenate(pair, axis=0), q_nope[p], TN).astype(BF16))
+            d_all.extend(pair)
+        d_rope = dot(jnp.concatenate(d_all, axis=0), q_rope[...], TN)
         d_latent = dot(jnp.concatenate(d_nope, axis=1), key_weight[...], NT)
         d_latent = d_latent + dot(jnp.concatenate(d_value, axis=1), value_weight[...], NT)
         part[step, :, :, :, 0:D_LAT] = d_latent.astype(BF16).reshape(4, 4, PIECE, D_LAT)
         part[step, :, :, :, D_LAT:WIDE] = d_rope.astype(BF16).reshape(4, 4, PIECE, WIDE - D_LAT)
 
-        for turn in range(4):
-
-            @pl.when(step == BACK_STEP[1, turn])
+    def backward(pair, carry):
+        chunk_grads(2 * pair)
+        chunk_grads(2 * pair + 1)
+        for turn in (3, 2, 1, 0):
+
+            @pl.when(pair == BACK_STEP[1, turn] // 2)
             def _(turn=turn):
                 t_copy(turn).start()
 
-            @pl.when(step == BACK_STEP[0, turn])
+        for turn in (3, 2, 1, 0):
+
+            @pl.when(pair == BACK_STEP[0, turn] // 2)
             def _(turn=turn):
                 add_own(turn)
 
         return carry
 
-    lax.fori_loop(0, CHUNKS, backward, 0)
+    lax.fori_loop(0, CHUNKS // 2, backward, 0)
     add_last(3)
     add_last(2)
 
@@ -427,12 +464,11 @@
 
     lax.fori_loop(0, CHUNKS, to_queries, 0)
     for h in range(MAPS):
-        query_grad[:, h * D_QK : (h + 1) * D_QK] = (q_acc[h, :, 0:D_QK] * LOGIT_SCALE).astype(BF16)
+        query_grad[:, h * D_QK : (h + 1) * D_QK] = q_acc[h, :, 0:D_QK].astype(BF16)
 
     stores = [
         pltpu.make_async_copy(query_grad, query_hbm, out_sem.at[0]),
-        pltpu.make_async_copy(latent_out, latent_out_hbm, out_sem.at[1]),
-        pltpu.make_async_copy(rope_out, rope_out_hbm, out_sem.at[2]),
+        pltpu.make_async_copy(result, result_hbm, out_sem.at[1]),
     ]
     stores[0].start()
     z_mine = me.zh * 2 + me.zl
@@ -458,6 +494,24 @@
         else:
             own_y.start()
 
+    @pl.when(me.c == 0)
+    def _():
+        for i in range(3):
+            rows_copy(i).wait_send()
+
+    @pl.when(me.c == 1)
+    def _():
+        for i in range(3):
+            piece_copy(i).wait_send()
+        for turn in range(4):
+            for d in (1, 2, 3):
+                f_copy(turn, d).wait_send()
+
+    early = [s_copy(turn) for turn in range(4)] + [t_copy(turn) for turn in range(4)]
+    early += [l_copy(turn, d) for turn in (0, 2, 3) for d in (1, 2, 3)]
+    early += [p_copy(turn, d) for turn in (3, 2) for d in (1, 2, 3)]
+    for copy in early:
+        copy.wait_send()
     add_first(3)
     add_first(2)
     add_last(1)
@@ -471,54 +525,54 @@
         remote(there, there, y_send.at[0], y_recv.at[z], z_line[0]).wait_recv()
     place = me.c * 4 + me.y
     result[place] = total_of([from_z[z] for z in range(8)]).astype(BF16)
-    ends = y_lines + [sibling]
-
-    def e_copy(i):
-        return remote(result.at[place], result.at[place], e_send.at[i], e_recv.at[place], ends[i])
-
-    for i in (2, 3, 0, 1, 4, 5, 6):
-        e_copy(i).start()
-    for d in range(1, 8):
-        there = result.at[lax.rem(place + d, 8)]
-        remote(there, there, e_send.at[0], e_recv.at[lax.rem(place + d, 8)], sibling).wait_recv()
-    everything = result[...].reshape(ROWS, WIDE)
-    latent_out[...] = everything[:, 0:D_LAT]
-    rope_out[...] = everything[:, D_LAT:WIDE].astype(F32).T[0:D_ROPE].astype(BF16)
+
+    def e_copy(d):
+        piece = result.at[place]
+        return remote(piece, piece, e_send.at[d - 1], e_recv.at[d - 1], y_line[d - 1])
+
+    def r_copy(d):
+        piece = result.at[me.c * 4 + lax.rem(me.y + 4 - d, 4)]
+        return remote(piece, piece, r_send.at[d], r_recv.at[d], sibling)
+
+    for d in (2, 1, 3):
+        e_copy(d).start()
+    r_copy(0).start()
+    for d in (1, 3, 2):
+        e_copy(d).wait_recv()
+        r_copy(d).start()
+    for d in range(4):
+        r_copy(d).wait_recv()
     stores[1].start()
-    stores[2].start()
-
-    @pl.when(me.c == 0)
-    def _():
-        for i in range(3):
-            rows_copy(i).wait_send()
-
-    @pl.when(me.c == 1)
-    def _():
-        for i in range(3):
-            piece_copy(i).wait_send()
-        for turn in range(4):
-            for d in (1, 2, 3):
-                f_copy(turn, d).wait_send()
-
-    sent = [s_copy(turn) for turn in range(4)] + [t_copy(turn) for turn in range(4)]
-    sent += [make(turn, d) for make in (l_copy, p_copy, g_copy) for turn in range(4) for d in (1, 2, 3)]
+    sent = [p_copy(turn, d) for turn in (1, 0) for d in (1, 2, 3)]
+    sent += [g_copy(turn, d) for turn in range(4) for d in (1, 2, 3)]
     sent += [y_copy(turn, zl) for turn in (1, 2, 3) for zl in (0, 1)] + [own_y]
-    sent += [e_copy(i) for i in range(7)]
+    sent += [e_copy(d) for d in (1, 2, 3)] + [r_copy(d) for d in range(4)]
     for copy in sent:
         copy.wait_send()
     for store in stores:
         store.wait()
 
 
-def copy_out(query_in, latent_in, rope_in, query_out, latent_out, rope_out, query, latent, rope, in_sem, out_sem):
-    steps = [(query_in, query, query_out), (latent_in, latent, latent_out), (rope_in, rope, rope_out)]
-    reads = [pltpu.make_async_copy(a, b, in_sem.at[i]) for i, (a, b, c) in enumerate(steps)]
-    writes = [pltpu.make_async_copy(b, c, out_sem.at[i]) for i, (a, b, c) in enumerate(steps)]
+def copy_out(query_in, result_in, query_out, latent_out, rope_out, query, result, latent, rope, in_sem, out_sem):
+    reads = [
+        pltpu.make_async_copy(result_in, result, in_sem.at[0]),
+        pltpu.make_async_copy(query_in, query, in_sem.at[1]),
+    ]
+    writes = [
+        pltpu.make_async_copy(query, query_out, out_sem.at[0]),
+        pltpu.make_async_copy(latent, latent_out, out_sem.at[1]),
+        pltpu.make_async_copy(rope, rope_out, out_sem.at[2]),
+    ]
     for read in reads:
         read.start()
-    for read, write in zip(reads, writes):
-        read.wait()
-        write.start()
+    reads[0].wait()
+    everything = result[...].reshape(ROWS, WIDE)
+    rope[...] = everything[:, D_LAT:WIDE].astype(F32).T[0:D_ROPE].astype(BF16)
+    writes[2].start()
+    latent[...] = everything[:, 0:D_LAT]
+    writes[1].start()
+    reads[1].wait()
+    writes[0].start()
     for write in writes:
         write.wait()
 
@@ -540,11 +594,11 @@
     piece = (PIECE, WIDE)
     outs = pl.pallas_call(
         fused_kernel,
-        out_shape=OUTS,
+        out_shape=(OUTS[0], jax.ShapeDtypeStruct((8,) + piece, BF16)),
         in_specs=[ANY] * 9,
-        out_specs=(ANY, ANY, ANY),
-        scratch_shapes=[pltpu.VMEM(out.shape, BF16) for out in OUTS]
-        + [
+        out_specs=(ANY, ANY),
+        scratch_shapes=[
+            pltpu.VMEM((ROWS, MAPS * D_QK), BF16),
             pltpu.SMEM((PAIRS_DEV,), F32),
             pltpu.SMEM((32,), jnp.int32),
             pltpu.VMEM((1, 512), F32),
@@ -558,6 +612,8 @@
             pltpu.VMEM((CHUNKS, CHUNK), jnp.int32),
             pltpu.VMEM((ROWS, CHUNK), jnp.int32),
             pltpu.VMEM((MAPS, ROWS, 256), BF16),
+            pltpu.VMEM((PAIRS_DEV, 2 * ROWS, 2 * D_NOPE), BF16),
+            pltpu.VMEM((MAPS * ROWS, 128), BF16),
             pltpu.VMEM((CHUNKS, MAPS, CHUNK, 256), BF16),
             pltpu.VMEM((CHUNKS, PAIRS_DEV, CHUNK, PAIR_WIDTH), BF16),
             pltpu.VMEM((CHUNKS, MAPS, ROWS, CHUNK), F32),
@@ -578,7 +634,7 @@
             pltpu.VMEM((8,) + piece, BF16),
             pltpu.VMEM((8,) + piece, BF16),
         ]
-        + [DMA((n,)) for n in (9, 3, 12, 12, 3, 4, 12, 12, 4, 4, 4, 4, 12, 12, 12, 12, 8, 8, 7, 8)],
+        + [DMA((n,)) for n in (9, 2, 12, 12, 3, 4, 12, 12, 4, 4, 4, 4, 12, 12, 12, 12, 8, 8, 3, 3, 4, 4)],
         compiler_params=pltpu.CompilerParams(
             collective_id=0, has_side_effects=True, vmem_limit_bytes=56 << 20
         ),
@@ -587,9 +643,11 @@
     return pl.pallas_call(
         copy_out,
         out_shape=OUTS,
-        in_specs=[ANY] * 3,
+        in_specs=[ANY] * 2,
         out_specs=(ANY, ANY, ANY),
-        scratch_shapes=[pltpu.VMEM(out.shape, BF16) for out in OUTS] + [DMA((3,)), DMA((3,))],
+        scratch_shapes=[pltpu.VMEM(OUTS[0].shape, BF16), pltpu.VMEM((8,) + piece, BF16)]
+        + [pltpu.VMEM(out.shape, BF16) for out in OUTS[1:]]
+        + [DMA((2,)), DMA((3,))],
         name="copy_out",
     )(*outs)
 

time: 58 us -> 56.9 us (0.981)
  Pallas kernels: 57.3 us -> 56.1 us
    pallas_call x2, Pallas kernels: 57.3 us -> 56.1 us  [the longest x1 54.3 us: fused(): pl.pallas_call(fused_kernel, out_shape=(OUTS[0], jax.ShapeDtypeStruct((8,...]
where the time goes in v4:
time: 56.9 us; the launch traced here: 56.7 us
  Pallas kernels  56.1 us (99%)
  between operations  0.64 us (1%)
    pallas_call x1, Pallas kernels, fused(): pl.pallas_call(fused_kernel, out_shape=(OUTS[0], jax.ShapeDtypeStruct((8,...  54.3 us
    pallas_call x1, Pallas kernels, fused(): pl.pallas_call(copy_out, out_shape=OUTS, in_specs=[ANY] * 2, out_specs=(A...  1.77 us

profile of v4, /device:TPU:1, one launch (start us, length us, event | category | flops | bytes accessed | tf_op | source)
XLA Modules:
  0.0 56.7 jit_solution(9683175109378175568)
XLA Ops:
  0.6 54.3 %fused.1 = (bf16[128,768]{1,0:T(8,128)(2,1)}, bf16[8,16,640]{2,1,0:T(8,128)(2,1)}) custom-call(f32[2]{0:T(128)} %lam_hbm.1, s32[32]{0:T(128)} %order_hbm.1, f32[1,512]{1,0:T(1,128)} %bitcast.6, bf16[128,768]{1,0:T(8,128)(2,1)} %queries_hbm.1, bf16[8,16,512]{2,1,0:T(8,128)(2,1)} %bitcast.4, bf16[64,128]{1,0:T(8,128)(2,1)} %bitcast.5, ...), custom_call_target="tpu_custom_call" | custom-call | tf_op jit(solution)/shard_map/fused/pallas_call | solution.py:595
  55.0 1.8 %copy_out.1 = (bf16[128,768]{1,0:T(8,128)(2,1)}, bf16[128,512]{1,0:T(8,128)(2,1)}, bf16[64,128]{1,0:T(8,128)(2,1)}) custom-call(bf16[128,768]{1,0:T(8,128)(2,1)} %get-tuple-element.8.query_in, bf16[8,16,640]{2,1,0:T(8,128)(2,1)} %get-tuple-element.9.result_in), custom_call_target="tpu_custom_call" | custom-call | tf_op jit(solution)/shard_map/copy_out/pallas_call | solution.py:643

commit v5 on v4

--- a/solution.py
+++ b/solution.py
@@ -105,11 +105,11 @@
 
 def fused_kernel(
     lam_hbm, order_hbm, gain_hbm, queries_hbm, latent_hbm, rope_hbm, key_weight_hbm, value_weight_hbm, out_grad_hbm,
-    query_hbm, result_hbm,
-    query_grad, lam, block_order, gain, queries, rope_in, rope_rows, key_weight, value_weight, out_grad,
+    query_grad, result,
+    lam, block_order, gain, queries, rope_in, rope_rows, key_weight, value_weight, out_grad,
     keys, key_pos, query_pos, q_cat, q_nope, q_rope, k_cat, values, scores, d_scores, tops, tops_then, outs, totals, lowered, deltas, q_acc,
-    part, from_s, from_l, middle, from_f, small, from_z, result,
-    in_sem, out_sem, f_send, f_recv, z_send, z_recv, l_send, l_recv, s_send, s_recv,
+    part, from_s, from_l, middle, from_f, small, from_z,
+    in_sem, f_send, f_recv, z_send, z_recv, l_send, l_recv, s_send, s_recv,
     t_send, t_recv, p_send, p_recv, g_send, g_recv, y_send, y_recv, e_send, e_recv, r_send, r_recv,
 ):
     me = Place()
@@ -121,10 +121,6 @@
     firsts = {d: me.first_peer(d) for d in (1, 2, 3)}
     lasts = {d: me.last_peer(d) for d in (1, 2, 3)}
     sibling = me.sibling()
-    barrier = pltpu.get_barrier_semaphore()
-    for device in x_line + y_line + z_line + [sibling]:
-        pl.semaphore_signal(barrier, inc=1, device_id=device, device_id_type=MESH)
-
     near = lax.rem(me.zh + 3 - 2 * me.zl, 4)
     z_order = [me.zh, near, lax.rem(me.zh + 1 + 2 * me.zl, 4), lax.rem(me.zh + 2, 4)]
     my_rows = keys.at[base + me.zh, me.last]
@@ -155,6 +151,10 @@
         piece_load.start()
 
     loads[2].start()
+    barrier = pltpu.get_barrier_semaphore()
+    greeted = [z_line[i] for i in (3, 2, 4, 1, 5)] + [x_line[1], y_line[1], z_line[0], z_line[6]]
+    for device in greeted + [x_line[0], x_line[2], y_line[0], y_line[2], sibling]:
+        pl.semaphore_signal(barrier, inc=1, device_id=device, device_id_type=MESH)
     loads[0].start()
     loads[1].start()
     for load in loads[3:]:
@@ -390,7 +390,7 @@
     def add_own(turn):
         t_copy(turn).wait_recv()
         there = part.at[BACK_STEP[0, turn]]
-        there[...] = total_of([there[...], from_s[turn]]).astype(BF16)
+        there[...] += from_s[turn]
         for d in (2, 1, 3):
             p_copy(turn, d).start()
 
@@ -466,11 +466,6 @@
     for h in range(MAPS):
         query_grad[:, h * D_QK : (h + 1) * D_QK] = q_acc[h, :, 0:D_QK].astype(BF16)
 
-    stores = [
-        pltpu.make_async_copy(query_grad, query_hbm, out_sem.at[0]),
-        pltpu.make_async_copy(result, result_hbm, out_sem.at[1]),
-    ]
-    stores[0].start()
     z_mine = me.zh * 2 + me.zl
 
     def y_copy(turn, zl):
@@ -542,37 +537,26 @@
         r_copy(d).start()
     for d in range(4):
         r_copy(d).wait_recv()
-    stores[1].start()
     sent = [p_copy(turn, d) for turn in (1, 0) for d in (1, 2, 3)]
     sent += [g_copy(turn, d) for turn in range(4) for d in (1, 2, 3)]
     sent += [y_copy(turn, zl) for turn in (1, 2, 3) for zl in (0, 1)] + [own_y]
     sent += [e_copy(d) for d in (1, 2, 3)] + [r_copy(d) for d in range(4)]
     for copy in sent:
         copy.wait_send()
-    for store in stores:
-        store.wait()
-
-
-def copy_out(query_in, result_in, query_out, latent_out, rope_out, query, result, latent, rope, in_sem, out_sem):
-    reads = [
-        pltpu.make_async_copy(result_in, result, in_sem.at[0]),
-        pltpu.make_async_copy(query_in, query, in_sem.at[1]),
+
+
+def copy_out(query, result, query_out, latent_out, rope_out, latent, rope, sem):
+    writes = [
+        pltpu.make_async_copy(query, query_out, sem.at[0]),
+        pltpu.make_async_copy(latent, latent_out, sem.at[1]),
+        pltpu.make_async_copy(rope, rope_out, sem.at[2]),
     ]
-    writes = [
-        pltpu.make_async_copy(query, query_out, out_sem.at[0]),
-        pltpu.make_async_copy(latent, latent_out, out_sem.at[1]),
-        pltpu.make_async_copy(rope, rope_out, out_sem.at[2]),
-    ]
-    for read in reads:
-        read.start()
-    reads[0].wait()
+    writes[0].start()
     everything = result[...].reshape(ROWS, WIDE)
     rope[...] = everything[:, D_LAT:WIDE].astype(F32).T[0:D_ROPE].astype(BF16)
     writes[2].start()
     latent[...] = everything[:, 0:D_LAT]
     writes[1].start()
-    reads[1].wait()
-    writes[0].start()
     for write in writes:
         write.wait()
 
@@ -580,6 +564,7 @@
 VMEM = pl.BlockSpec(memory_space=pltpu.VMEM)
 SMEM = pl.BlockSpec(memory_space=pltpu.SMEM)
 ANY = pl.BlockSpec(memory_space=pl.ANY)
+HBM = pl.BlockSpec(memory_space=pltpu.HBM)
 DMA = pltpu.SemaphoreType.DMA
 
 
@@ -594,11 +579,10 @@
     piece = (PIECE, WIDE)
     outs = pl.pallas_call(
         fused_kernel,
-        out_shape=(OUTS[0], jax.ShapeDtypeStruct((8,) + piece, BF16)),
-        in_specs=[ANY] * 9,
-        out_specs=(ANY, ANY),
+        out_shape=(pltpu.VMEM(OUTS[0].shape, BF16), pltpu.VMEM((8,) + piece, BF16)),
+        in_specs=[HBM] * 9,
+        out_specs=(VMEM, VMEM),
         scratch_shapes=[
-            pltpu.VMEM((ROWS, MAPS * D_QK), BF16),
             pltpu.SMEM((PAIRS_DEV,), F32),
             pltpu.SMEM((32,), jnp.int32),
             pltpu.VMEM((1, 512), F32),
@@ -632,24 +616,21 @@
             pltpu.VMEM((4, 3) + piece, BF16),
             pltpu.VMEM((4,) + piece, BF16),
             pltpu.VMEM((8,) + piece, BF16),
-            pltpu.VMEM((8,) + piece, BF16),
         ]
-        + [DMA((n,)) for n in (9, 2, 12, 12, 3, 4, 12, 12, 4, 4, 4, 4, 12, 12, 12, 12, 8, 8, 3, 3, 4, 4)],
+        + [DMA((n,)) for n in (9, 12, 12, 3, 4, 12, 12, 4, 4, 4, 4, 12, 12, 12, 12, 8, 8, 3, 3, 4, 4)],
         compiler_params=pltpu.CompilerParams(
             collective_id=0, has_side_effects=True, vmem_limit_bytes=56 << 20
         ),
         name="fused",
-    )(*operands)
+    )(*(pltpu.with_memory_space_constraint(operand, pltpu.HBM) for operand in operands))
     return pl.pallas_call(
         copy_out,
         out_shape=OUTS,
-        in_specs=[ANY] * 2,
-        out_specs=(ANY, ANY, ANY),
-        scratch_shapes=[pltpu.VMEM(OUTS[0].shape, BF16), pltpu.VMEM((8,) + piece, BF16)]
-        + [pltpu.VMEM(out.shape, BF16) for out in OUTS[1:]]
-        + [DMA((2,)), DMA((3,))],
+        in_specs=[VMEM] * 2,
+        out_specs=(HBM, HBM, HBM),
+        scratch_shapes=[pltpu.VMEM(out.shape, BF16) for out in OUTS[1:]] + [DMA((3,))],
         name="copy_out",
-    )(*outs)
+    )(*(pltpu.with_memory_space_constraint(out, pltpu.VMEM) for out in outs))
 
 
 def on_device(

time: 56.9 us -> 55.2 us (0.970)
  Pallas kernels: 56.1 us -> 54.5 us
    pallas_call x2, Pallas kernels: 56.1 us -> 54.5 us  [the longest x1 53.7 us: fused(): pl.pallas_call(fused_kernel, out_shape=(pltpu.VMEM(OUTS[0].shape, BF16),...]
where the time goes in v5:
time: 55.2 us; the launch traced here: 55.1 us
  Pallas kernels  54.5 us (99%)
  between operations  0.64 us (1%)
    pallas_call x1, Pallas kernels, fused(): pl.pallas_call(fused_kernel, out_shape=(pltpu.VMEM(OUTS[0].shape, BF16),...  53.7 us

profile of v5, /device:TPU:1, one launch (start us, length us, event | category | flops | bytes accessed | tf_op | source)
XLA Modules:
  0.0 55.1 jit_solution(1310283292715215281)
XLA Ops:
  0.6 53.7 %fused.1 = (bf16[128,768]{1,0:T(8,128)(2,1)S(1)}, bf16[8,16,640]{2,1,0:T(8,128)(2,1)S(1)}) custom-call(f32[2]{0:T(128)} %lam_hbm.1, s32[32]{0:T(128)} %order_hbm.1, f32[1,512]{1,0:T(1,128)} %bitcast.6, bf16[128,768]{1,0:T(8,128)(2,1)} %queries_hbm.1, bf16[8,16,512]{2,1,0:T(8,128)(2,1)} %bitcast.4, bf16[64,128]{1,0:T(8,128)(2,1)} %bitcast.5, ...), custom_call_target="tpu_custom_call" | custom-call | tf_op jit(solution)/shard_map/fused/pallas_call | solution.py:580
  54.3 0.8 %copy_out.1 = (bf16[128,768]{1,0:T(8,128)(2,1)}, bf16[128,512]{1,0:T(8,128)(2,1)}, bf16[64,128]{1,0:T(8,128)(2,1)}) custom-call(bf16[128,768]{1,0:T(8,128)(2,1)S(1)} %get-tuple-element.8.query, bf16[8,16,640]{2,1,0:T(8,128)(2,1)S(1)} %get-tuple-element.9.result), custom_call_target="tpu_custom_call" | custom-call | tf_op jit(solution)/shard_map/copy_out/pallas_call | solution.py:626

commit v6 on v5

--- a/solution.py
+++ b/solution.py
@@ -108,7 +108,7 @@
     query_grad, result,
     lam, block_order, gain, queries, rope_in, rope_rows, key_weight, value_weight, out_grad,
     keys, key_pos, query_pos, q_cat, q_nope, q_rope, k_cat, values, scores, d_scores, tops, tops_then, outs, totals, lowered, deltas, q_acc,
-    part, from_s, from_l, middle, from_f, small, from_z,
+    part, from_s, from_l, middle, from_f, small, from_z, from_far,
     in_sem, f_send, f_recv, z_send, z_recv, l_send, l_recv, s_send, s_recv,
     t_send, t_recv, p_send, p_recv, g_send, g_recv, y_send, y_recv, e_send, e_recv, r_send, r_recv,
 ):
@@ -152,7 +152,7 @@
 
     loads[2].start()
     barrier = pltpu.get_barrier_semaphore()
-    greeted = [z_line[i] for i in (3, 2, 4, 1, 5)] + [x_line[1], y_line[1], z_line[0], z_line[6]]
+    greeted = [z_line[i] for i in (2, 4, 1, 5)] + [x_line[1], y_line[1], z_line[0], z_line[6]]
     for device in greeted + [x_line[0], x_line[2], y_line[0], y_line[2], sibling]:
         pl.semaphore_signal(barrier, inc=1, device_id=device, device_id_type=MESH)
     loads[0].start()
@@ -174,7 +174,7 @@
         piece_load.wait()
         my_piece[:, D_LAT:WIDE] = rope_rows[4 + me.y]
 
-    pl.semaphore_wait(barrier, 14)
+    pl.semaphore_wait(barrier, 13)
 
     z_to = [
         me.at(zh=near, zl=1 - me.zl),
@@ -327,21 +327,19 @@
             l_copy(turn, d).wait_recv()
         s_copy(turn).start()
 
+    @pl.when(me.c == 0)
+    def _():
+        rows_wait(3)
+
+    @pl.when(me.c == 1)
+    def _():
+        for d in (1, 3, 2):
+            f_copy(3, d).wait_recv()
+
+    l_sends(3)
+
     own_ready(0)
     absorb([base + z_order[0]])
-
-    @pl.when(me.c == 0)
-    def _():
-        rows_wait(3)
-
-    @pl.when(me.c == 1)
-    def _():
-        for d in (1, 3, 2):
-            f_copy(3, d).wait_recv()
-
-    for d in (2, 1, 3):
-        l_copy(1, d).wait_send()
-    l_sends(3)
 
     def expand(turn, carry):
         own_ready(turn)
@@ -445,7 +443,7 @@
             def _(turn=turn):
                 t_copy(turn).start()
 
-        for turn in (3, 2, 1, 0):
+        for turn in (3, 2):
 
             @pl.when(pair == BACK_STEP[0, turn] // 2)
             def _(turn=turn):
@@ -453,7 +451,19 @@
 
         return carry
 
-    lax.fori_loop(0, CHUNKS // 2, backward, 0)
+    lax.fori_loop(0, 3, backward, 0)
+
+    def backward_last(step, carry):
+        chunk_grads(step)
+
+        @pl.when(step == 6)
+        def _():
+            add_own(1)
+
+        return carry
+
+    lax.fori_loop(6, 8, backward_last, 0)
+    add_own(0)
     add_last(3)
     add_last(2)
 
@@ -473,8 +483,11 @@
         device = me.at(zh=z_order[turn], zl=zl)
         return remote(small.at[turn], from_z.at[z_mine], y_send.at[i], y_recv.at[z_mine], device)
 
+    far_y = remote(
+        small.at[3], from_far, y_send.at[6], y_recv.at[8], me.at(zh=z_order[3], zl=1 - me.zl)
+    )
     own_y = remote(
-        small.at[0], from_z.at[z_mine], y_send.at[0], y_recv.at[z_mine], me.at(zl=1 - me.zl)
+        from_z.at[z_mine], from_z.at[z_mine], y_send.at[0], y_recv.at[z_mine], me.at(zl=1 - me.zl)
     )
 
     def add_first(turn):
@@ -483,10 +496,14 @@
         small[turn] = total_of(
             [middle[turn, me.first]] + [from_f[turn, d] for d in range(3)]
         ).astype(BF16)
-        if turn:
+        if turn == 3:
+            far_y.start()
+        elif turn:
             for zl in (0, 1):
                 y_copy(turn, zl).start()
         else:
+            far_y.wait_recv()
+            from_z[z_mine] = total_of([small[0], from_far[...]]).astype(BF16)
             own_y.start()
 
     @pl.when(me.c == 0)
@@ -503,7 +520,7 @@
                 f_copy(turn, d).wait_send()
 
     early = [s_copy(turn) for turn in range(4)] + [t_copy(turn) for turn in range(4)]
-    early += [l_copy(turn, d) for turn in (0, 2, 3) for d in (1, 2, 3)]
+    early += [l_copy(turn, d) for turn in range(4) for d in (1, 2, 3)]
     early += [p_copy(turn, d) for turn in (3, 2) for d in (1, 2, 3)]
     for copy in early:
         copy.wait_send()
@@ -513,13 +530,12 @@
     add_last(0)
     add_first(1)
     add_first(0)
-    from_z[z_mine] = small[0]
-    for d in range(1, 8):
-        z = lax.rem(z_mine + d, 8)
-        there = from_z.at[z]
-        remote(there, there, y_send.at[0], y_recv.at[z], z_line[0]).wait_recv()
+    told = [lax.rem(me.zh + k, 4) * 2 + zl for k in (0, 1, 3) for zl in (0, 1)]
+    remote(small.at[0], from_z.at[0], y_send.at[0], y_recv.at[lax.rem(z_mine + 1 - 2 * me.zl + 8, 8)], z_line[0]).wait_recv()
+    for z in told[2:]:
+        remote(small.at[0], from_z.at[0], y_send.at[0], y_recv.at[z], z_line[0]).wait_recv()
     place = me.c * 4 + me.y
-    result[place] = total_of([from_z[z] for z in range(8)]).astype(BF16)
+    result[place] = total_of([from_z[z] for z in told]).astype(BF16)
 
     def e_copy(d):
         piece = result.at[place]
@@ -532,16 +548,17 @@
     for d in (2, 1, 3):
         e_copy(d).start()
     r_copy(0).start()
+    sent = [p_copy(turn, d) for turn in (1, 0) for d in (1, 2, 3)]
+    sent += [g_copy(turn, d) for turn in range(4) for d in (1, 2, 3)]
+    sent += [y_copy(turn, zl) for turn in (1, 2) for zl in (0, 1)] + [far_y, own_y]
+    for copy in sent:
+        copy.wait_send()
     for d in (1, 3, 2):
         e_copy(d).wait_recv()
         r_copy(d).start()
     for d in range(4):
         r_copy(d).wait_recv()
-    sent = [p_copy(turn, d) for turn in (1, 0) for d in (1, 2, 3)]
-    sent += [g_copy(turn, d) for turn in range(4) for d in (1, 2, 3)]
-    sent += [y_copy(turn, zl) for turn in (1, 2, 3) for zl in (0, 1)] + [own_y]
-    sent += [e_copy(d) for d in (1, 2, 3)] + [r_copy(d) for d in range(4)]
-    for copy in sent:
+    for copy in [e_copy(d) for d in (1, 2, 3)] + [r_copy(d) for d in range(4)]:
         copy.wait_send()
 
 
@@ -616,8 +633,9 @@
             pltpu.VMEM((4, 3) + piece, BF16),
             pltpu.VMEM((4,) + piece, BF16),
             pltpu.VMEM((8,) + piece, BF16),
+            pltpu.VMEM(piece, BF16),
         ]
-        + [DMA((n,)) for n in (9, 12, 12, 3, 4, 12, 12, 4, 4, 4, 4, 12, 12, 12, 12, 8, 8, 3, 3, 4, 4)],
+        + [DMA((n,)) for n in (9, 12, 12, 3, 4, 12, 12, 4, 4, 4, 4, 12, 12, 12, 12, 8, 9, 3, 3, 4, 4)],
         compiler_params=pltpu.CompilerParams(
             collective_id=0, has_side_effects=True, vmem_limit_bytes=56 << 20
         ),

time: 55.2 us -> 54.5 us (0.987)
  Pallas kernels: 54.5 us -> 53.7 us
    pallas_call x1, Pallas kernels: 53.7 us -> 53 us  [fused(): pl.pallas_call(fused_kernel, out_shape=(pltpu.VMEM(OUTS[0].shape, BF16),...]
where the time goes in v6:
time: 54.5 us; the launch traced here: 54.4 us
  Pallas kernels  53.7 us (99%)
  between operations  0.64 us (1%)
    pallas_call x1, Pallas kernels, fused(): pl.pallas_call(fused_kernel, out_shape=(pltpu.VMEM(OUTS[0].shape, BF16),...  53 us

profile of v6, /device:TPU:1, one launch (start us, length us, event | category | flops | bytes accessed | tf_op | source)
XLA Modules:
  0.0 54.4 jit_solution(2089573127478654947)
XLA Ops:
  0.6 53.0 %fused.1 = (bf16[128,768]{1,0:T(8,128)(2,1)S(1)}, bf16[8,16,640]{2,1,0:T(8,128)(2,1)S(1)}) custom-call(f32[2]{0:T(128)} %lam_hbm.1, s32[32]{0:T(128)} %order_hbm.1, f32[1,512]{1,0:T(1,128)} %bitcast.6, bf16[128,768]{1,0:T(8,128)(2,1)} %queries_hbm.1, bf16[8,16,512]{2,1,0:T(8,128)(2,1)} %bitcast.4, bf16[64,128]{1,0:T(8,128)(2,1)} %bitcast.5, ...), custom_call_target="tpu_custom_call" | custom-call | tf_op jit(solution)/shard_map/fused/pallas_call | solution.py:597
  53.6 0.8 %copy_out.1 = (bf16[128,768]{1,0:T(8,128)(2,1)}, bf16[128,512]{1,0:T(8,128)(2,1)}, bf16[64,128]{1,0:T(8,128)(2,1)}) custom-call(bf16[128,768]{1,0:T(8,128)(2,1)S(1)} %get-tuple-element.8.query, bf16[8,16,640]{2,1,0:T(8,128)(2,1)S(1)} %get-tuple-element.9.result), custom_call_target="tpu_custom_call" | custom-call | tf_op jit(solution)/shard_map/copy_out/pallas_call | solution.py:644

commit v7 on v6

--- a/solution.py
+++ b/solution.py
@@ -117,6 +117,7 @@
     base, other = me.c * 4, me.o * 4
     x_line = [me.at(x=lax.rem(me.x + d, 4)) for d in (1, 2, 3)]
     y_line = [me.at(y=lax.rem(me.y + d, 4)) for d in (1, 2, 3)]
+    y_over = me.at(y=lax.rem(me.y + 2, 4), c=me.o)
     z_line = [me.z_peer(d) for d in range(1, 8)]
     firsts = {d: me.first_peer(d) for d in (1, 2, 3)}
     lasts = {d: me.last_peer(d) for d in (1, 2, 3)}
@@ -152,7 +153,7 @@
 
     loads[2].start()
     barrier = pltpu.get_barrier_semaphore()
-    greeted = [z_line[i] for i in (2, 4, 1, 5)] + [x_line[1], y_line[1], z_line[0], z_line[6]]
+    greeted = [z_line[i] for i in (2, 4, 1, 5)] + [x_line[1], y_line[1], y_over, z_line[0], z_line[6]]
     for device in greeted + [x_line[0], x_line[2], y_line[0], y_line[2], sibling]:
         pl.semaphore_signal(barrier, inc=1, device_id=device, device_id_type=MESH)
     loads[0].start()
@@ -174,7 +175,7 @@
         piece_load.wait()
         my_piece[:, D_LAT:WIDE] = rope_rows[4 + me.y]
 
-    pl.semaphore_wait(barrier, 13)
+    pl.semaphore_wait(barrier, 14)
 
     z_to = [
         me.at(zh=near, zl=1 - me.zl),
@@ -228,7 +229,7 @@
 
     @pl.when(me.c == 0)
     def _():
-        for i in range(3):
+        for i in range(2):
             rows_copy(i).start()
         l_sends(0)
 
@@ -272,6 +273,9 @@
 
     @pl.when(me.c == 0)
     def _():
+        for i in range(2):
+            rows_copy(i).wait_send()
+        rows_copy(2).start()
         for turn in (1, 2):
             rows_wait(turn)
             l_sends(turn)
@@ -464,8 +468,6 @@
 
     lax.fori_loop(6, 8, backward_last, 0)
     add_own(0)
-    add_last(3)
-    add_last(2)
 
     def to_queries(i, carry):
         for h in range(MAPS):
@@ -506,10 +508,12 @@
             from_z[z_mine] = total_of([small[0], from_far[...]]).astype(BF16)
             own_y.start()
 
+    add_last(3)
+    add_last(2)
+
     @pl.when(me.c == 0)
     def _():
-        for i in range(3):
-            rows_copy(i).wait_send()
+        rows_copy(2).wait_send()
 
     @pl.when(me.c == 1)
     def _():
@@ -524,10 +528,10 @@
     early += [p_copy(turn, d) for turn in (3, 2) for d in (1, 2, 3)]
     for copy in early:
         copy.wait_send()
+    add_last(1)
     add_first(3)
+    add_last(0)
     add_first(2)
-    add_last(1)
-    add_last(0)
     add_first(1)
     add_first(0)
     told = [lax.rem(me.zh + k, 4) * 2 + zl for k in (0, 1, 3) for zl in (0, 1)]
@@ -539,13 +543,13 @@
 
     def e_copy(d):
         piece = result.at[place]
-        return remote(piece, piece, e_send.at[d - 1], e_recv.at[d - 1], y_line[d - 1])
+        return remote(piece, piece, e_send.at[d - 1], e_recv.at[d - 1], (y_line + [y_over])[d - 1])
 
     def r_copy(d):
         piece = result.at[me.c * 4 + lax.rem(me.y + 4 - d, 4)]
         return remote(piece, piece, r_send.at[d], r_recv.at[d], sibling)
 
-    for d in (2, 1, 3):
+    for d in (4, 2, 1, 3):
         e_copy(d).start()
     r_copy(0).start()
     sent = [p_copy(turn, d) for turn in (1, 0) for d in (1, 2, 3)]
@@ -553,12 +557,14 @@
     sent += [y_copy(turn, zl) for turn in (1, 2) for zl in (0, 1)] + [far_y, own_y]
     for copy in sent:
         copy.wait_send()
-    for d in (1, 3, 2):
+    for d in (1, 3):
         e_copy(d).wait_recv()
         r_copy(d).start()
-    for d in range(4):
+    for d in (2, 4):
+        e_copy(d).wait_recv()
+    for d in (0, 1, 3):
         r_copy(d).wait_recv()
-    for copy in [e_copy(d) for d in (1, 2, 3)] + [r_copy(d) for d in range(4)]:
+    for copy in [e_copy(d) for d in (1, 2, 3, 4)] + [r_copy(d) for d in (0, 1, 3)]:
         copy.wait_send()
 
 
@@ -635,7 +641,7 @@
             pltpu.VMEM((8,) + piece, BF16),
             pltpu.VMEM(piece, BF16),
         ]
-        + [DMA((n,)) for n in (9, 12, 12, 3, 4, 12, 12, 4, 4, 4, 4, 12, 12, 12, 12, 8, 9, 3, 3, 4, 4)],
+        + [DMA((n,)) for n in (9, 12, 12, 3, 4, 12, 12, 4, 4, 4, 4, 12, 12, 12, 12, 8, 9, 4, 4, 4, 4)],
         compiler_params=pltpu.CompilerParams(
             collective_id=0, has_side_effects=True, vmem_limit_bytes=56 << 20
         ),

time: 54.5 us -> 54.2 us (level)
  no operation moved by 1% of the time
where the time goes in v7:
time: 54.2 us; the launch traced here: 54 us
  Pallas kernels  53.4 us (99%)
  between operations  0.64 us (1%)
    pallas_call x1, Pallas kernels, fused(): pl.pallas_call(fused_kernel, out_shape=(pltpu.VMEM(OUTS[0].shape, BF16),...  52.6 us

profile of v7, /device:TPU:1, one launch (start us, length us, event | category | flops | bytes accessed | tf_op | source)
XLA Modules:
  0.0 54.0 jit_solution(5808624236931439106)
XLA Ops:
  0.6 52.6 %fused.1 = (bf16[128,768]{1,0:T(8,128)(2,1)S(1)}, bf16[8,16,640]{2,1,0:T(8,128)(2,1)S(1)}) custom-call(f32[2]{0:T(128)} %lam_hbm.1, s32[32]{0:T(128)} %order_hbm.1, f32[1,512]{1,0:T(1,128)} %bitcast.6, bf16[128,768]{1,0:T(8,128)(2,1)} %queries_hbm.1, bf16[8,16,512]{2,1,0:T(8,128)(2,1)} %bitcast.4, bf16[64,128]{1,0:T(8,128)(2,1)} %bitcast.5, ...), custom_call_target="tpu_custom_call" | custom-call | tf_op jit(solution)/shard_map/fused/pallas_call | solution.py:603
  53.3 0.8 %copy_out.1 = (bf16[128,768]{1,0:T(8,128)(2,1)}, bf16[128,512]{1,0:T(8,128)(2,1)}, bf16[64,128]{1,0:T(8,128)(2,1)}) custom-call(bf16[128,768]{1,0:T(8,128)(2,1)S(1)} %get-tuple-element.8.query, bf16[8,16,640]{2,1,0:T(8,128)(2,1)S(1)} %get-tuple-element.9.result), custom_call_target="tpu_custom_call" | custom-call | tf_op jit(solution)/shard_map/copy_out/pallas_call | solution.py:650

commit v8 on v7

--- a/solution.py
+++ b/solution.py
@@ -488,6 +488,10 @@
     far_y = remote(
         small.at[3], from_far, y_send.at[6], y_recv.at[8], me.at(zh=z_order[3], zl=1 - me.zl)
     )
+    mid_y = remote(
+        small.at[2], from_z.at[z_mine], y_send.at[4], y_recv.at[z_mine], me.at(zh=z_order[2])
+    )
+    z_mid = near * 2 + me.zl
     own_y = remote(
         from_z.at[z_mine], from_z.at[z_mine], y_send.at[0], y_recv.at[z_mine], me.at(zl=1 - me.zl)
     )
@@ -500,12 +504,15 @@
         ).astype(BF16)
         if turn == 3:
             far_y.start()
+        elif turn == 2:
+            mid_y.start()
         elif turn:
             for zl in (0, 1):
                 y_copy(turn, zl).start()
         else:
             far_y.wait_recv()
-            from_z[z_mine] = total_of([small[0], from_far[...]]).astype(BF16)
+            remote(small.at[0], from_z.at[0], y_send.at[0], y_recv.at[z_mid], z_line[0]).wait_recv()
+            from_z[z_mine] = total_of([small[0], from_far[...], from_z[z_mid]]).astype(BF16)
             own_y.start()
 
     add_last(3)
@@ -534,7 +541,7 @@
     add_first(2)
     add_first(1)
     add_first(0)
-    told = [lax.rem(me.zh + k, 4) * 2 + zl for k in (0, 1, 3) for zl in (0, 1)]
+    told = [lax.rem(me.zh + k, 4) * 2 + zl for k, zl in ((0, 0), (0, 1), (1, 0), (3, 1))]
     remote(small.at[0], from_z.at[0], y_send.at[0], y_recv.at[lax.rem(z_mine + 1 - 2 * me.zl + 8, 8)], z_line[0]).wait_recv()
     for z in told[2:]:
         remote(small.at[0], from_z.at[0], y_send.at[0], y_recv.at[z], z_line[0]).wait_recv()
@@ -554,7 +561,7 @@
     r_copy(0).start()
     sent = [p_copy(turn, d) for turn in (1, 0) for d in (1, 2, 3)]
     sent += [g_copy(turn, d) for turn in range(4) for d in (1, 2, 3)]
-    sent += [y_copy(turn, zl) for turn in (1, 2) for zl in (0, 1)] + [far_y, own_y]
+    sent += [y_copy(1, zl) for zl in (0, 1)] + [mid_y, far_y, own_y]
     for copy in sent:
         copy.wait_send()
     for d in (1, 3):

time: 54.2 us -> 54.4 us (level)
  no operation moved by 1% of the time
where the time goes in v8:
time: 54.4 us; the launch traced here: 54.3 us
  Pallas kernels  53.7 us (99%)
  between operations  0.64 us (1%)
    pallas_call x1, Pallas kernels, fused(): pl.pallas_call(fused_kernel, out_shape=(pltpu.VMEM(OUTS[0].shape, BF16),...  52.9 us

profile of v8, /device:TPU:1, one launch (start us, length us, event | category | flops | bytes accessed | tf_op | source)
XLA Modules:
  0.0 54.3 jit_solution(3644600166039200020)
XLA Ops:
  0.6 52.9 %fused.1 = (bf16[128,768]{1,0:T(8,128)(2,1)S(1)}, bf16[8,16,640]{2,1,0:T(8,128)(2,1)S(1)}) custom-call(f32[2]{0:T(128)} %lam_hbm.1, s32[32]{0:T(128)} %order_hbm.1, f32[1,512]{1,0:T(1,128)} %bitcast.6, bf16[128,768]{1,0:T(8,128)(2,1)} %queries_hbm.1, bf16[8,16,512]{2,1,0:T(8,128)(2,1)} %bitcast.4, bf16[64,128]{1,0:T(8,128)(2,1)} %bitcast.5, ...), custom_call_target="tpu_custom_call" | custom-call | tf_op jit(solution)/shard_map/fused/pallas_call | solution.py:610
  53.5 0.8 %copy_out.1 = (bf16[128,768]{1,0:T(8,128)(2,1)}, bf16[128,512]{1,0:T(8,128)(2,1)}, bf16[64,128]{1,0:T(8,128)(2,1)}) custom-call(bf16[128,768]{1,0:T(8,128)(2,1)S(1)} %get-tuple-element.8.query, bf16[8,16,640]{2,1,0:T(8,128)(2,1)S(1)} %get-tuple-element.9.result), custom_call_target="tpu_custom_call" | custom-call | tf_op jit(solution)/shard_map/copy_out/pallas_call | solution.py:657
